TPU v7x, 128 devices: a whole 4x4x4 slice. The times are simulated.
128 devices in a mesh: dp: 8 (over z, core), seq: 16 (over y, x).
Axes of the slice: x: 4, y: 4, z: 4, core: 2. Of those that a mesh axis runs over, the one named last changes fastest.
Arguments:
- seq_in: bfloat16 [8, 4096, 512], P('dp', 'seq'), may hold values from -6 to 6
- w_first: bfloat16 [5, 512, 512], replicated, may hold values from -0.125 to 0.125
- w_second: bfloat16 [5, 512, 1024], replicated, may hold values from -0.125 to 0.125
- head_vec: float32 [1024], replicated, may hold values from -5 to 5
- track_cot: bfloat16 [8, 2048, 1024], P('dp', 'seq'), may hold values from -6 to 6
- donor_pos: int32 [8, 256], P('dp', 'seq'), may hold values from 0 to 2047
- acceptor_pos: int32 [8, 256], P('dp', 'seq'), may hold values from 0 to 2047
- pair_cot: float32 [8, 256], P('dp', 'seq'), may hold values from -6 to 6
- live_pairs: int32 [8, 16], P('dp', 'seq'), may hold values from 1 to 16, 128 in all within a row
Outputs:
- scores: float32 [8, 256], P('dp', 'seq')
- grad_first: float32 [2560, 512], P(('dp', 'seq'))
- grad_second: float32 [2560, 1024], P(('dp', 'seq'))
- grad_input: bfloat16 [8, 4096, 512], P('dp', 'seq')
- grad_head: float32 [1024], replicated
Inputs may be any that keep to these rules, and one draw needn't show every extreme that they name: The first live_pairs[g, s] of device s's 16 slots are live, the rest are ignored; in each sequence the counts sum to half of all slots, and at least one device holds 16 live pairs.
All inputs are finite; a program needn't handle non-finite values.
Results may differ from a plain program's by a relative error of at most 0.015.
Values may be sent and summed in bfloat16 or wider, within the bound.
No kernel may reach another device: no remote copies, remote signals or barrier semaphores. Data moves between devices by JAX's collectives and lax.ppermute only.
A program may use at most 128 MiB of HBM per device.

v0:
```python
import jax
import jax.numpy as jnp
from jax import lax
from jax.experimental import pallas as pl
from jax.experimental.pallas import tpu as pltpu
from jax.sharding import PartitionSpec as P

BF = jnp.bfloat16
F32 = jnp.float32
ROOT = 0.7978845608028654
CUBE = 0.044715


def gelu_both(pre):
    square = pre * pre
    bent = jnp.tanh(ROOT * pre * (1.0 + CUBE * square))
    half = 0.5 * (1.0 + bent)
    slope = half + 0.5 * pre * (1.0 - bent * bent) * (ROOT * (1.0 + 3.0 * CUBE * square))
    return pre * half, slope


def dot(left, right, dims=((1,), (0,))):
    return lax.dot_general(left, right, (dims, ((), ())), preferred_element_type=F32)


VMEM = pl.BlockSpec(memory_space=pltpu.VMEM)
SMEM = pl.BlockSpec(memory_space=pltpu.SMEM)
HBM = pl.BlockSpec(memory_space=pltpu.HBM)
ANY = pl.BlockSpec(memory_space=pl.ANY)
MEBI = 1024 * 1024


def rounded(value):
    return value.astype(BF).astype(F32)


def half_lanes(rows):
    return lax.broadcasted_iota(jnp.int32, (rows, 128), 1) < 64


def swap(value):
    return pltpu.roll(value, 64, 1)


def started(moves, sems):
    copies = []
    for place, (source, target) in enumerate(moves):
        copies.append(pltpu.make_async_copy(source, target, sems.at[place]))
        copies[place].start()
    return copies


def wait_for(copies):
    for copy in copies:
        copy.wait()


def within(rows, seam, shift, seq_index):
    row = lax.broadcasted_iota(jnp.int32, (rows, 1), 0)
    return ((row >= seam) == (row + shift >= seam)) | (seq_index != 15)


def edge_kernel(inputs_hbm, track_hbm, out_hbm, rows_scr, track_scr, out_scr, sems):
    wait_for(
        started(
            [
                (inputs_hbm.at[pl.ds(0, 32)], rows_scr),
                (track_hbm.at[pl.ds(0, 16)], track_scr),
            ],
            sems,
        )
    )
    track = track_scr[...].astype(F32)
    pieces = [rows_scr[...].astype(F32)[:24]]
    for row in range(9):
        pieces += [track[row : row + 1, :512], track[row : row + 1, 512:]]
    pieces.append(jnp.zeros((6, 512), F32))
    out_scr[...] = jnp.concatenate(pieces, axis=0).astype(BF)
    wait_for(started([(out_scr, out_hbm)], sems))


def edges(inputs, track, count):
    first = pl.pallas_call(
        edge_kernel,
        out_shape=jax.ShapeDtypeStruct((48, 512), BF),
        in_specs=[HBM] * 2,
        out_specs=HBM,
        scratch_shapes=[
            pltpu.VMEM((32, 512), BF),
            pltpu.VMEM((16, 1024), BF),
            pltpu.VMEM((48, 512), BF),
            pltpu.SemaphoreType.DMA((2,)),
        ],
        compiler_params=pltpu.CompilerParams(vmem_limit_bytes=56 * MEBI),
        name="edges",
    )(inputs, track)
    return lax.ppermute(first, "seq", [(i, (i - 1) % count) for i in range(count)])


def forward_kernel(seq_ref, live_ref, *refs):
    sources, outs, held, staged, work = refs[:7], refs[7:11], refs[11:18], refs[18:22], refs[22:]
    inputs_ref, right_ref, first_mat, second_mat, donor_ref, accept_ref, cot_ref = held
    mess_ref, mine_ref, slope_1_ref, slope_2_ref = staged
    ext, act_scr, wide, sems, out_sems = work
    copies = started(list(zip(sources, held)), sems)

    def send(place):
        copy = pltpu.make_async_copy(staged[place], outs[place], out_sems.at[place])
        copy.start()
        return copy

    seq_index = seq_ref[0]
    ext[0:32, :] = jnp.zeros((32, 512), F32)
    ext[288:320, :] = jnp.zeros((32, 512), F32)
    wait_for(copies[:2])
    ext[20:276, :] = inputs_ref[...].astype(F32)
    ext[276:300, :] = right_ref[...].astype(F32)[:24]
    taps = jnp.concatenate(
        [
            jnp.where(within(288, 260, k - 2, seq_index), ext[14 + k : 302 + k, :], 0.0).astype(BF)
            for k in range(5)
        ],
        axis=1,
    )
    copies[2].wait()
    pre = dot(taps, first_mat[...])
    act, slope = gelu_both(pre)
    slope_1_ref[...] = slope
    sent = [send(2)]
    y_first = ext[16:304, :] + act
    for tile in range(4):
        lanes = slice(128 * tile, 128 * tile + 128)
        act_scr[288 * tile : 288 * tile + 288, :] = y_first[:, lanes]
        even = act_scr[pl.ds(288 * tile, 144, 2), :]
        wide[8:152, lanes] = even + act_scr[pl.ds(288 * tile + 1, 144, 2), :]
    pooled = 0.5 * wide[8:152, :]
    wide[0:8, :] = jnp.zeros((8, 512), F32)
    wide[152:160, :] = jnp.zeros((8, 512), F32)
    wide[8:152, :] = pooled
    mine_ref[0:256, :] = ext[32:288, :].astype(BF)
    mine_ref[256:384, :] = wide[16:144, :].astype(BF)
    sent.append(send(1))
    taps = jnp.concatenate(
        [
            jnp.where(within(144, 130, k - 2, seq_index), wide[6 + k : 150 + k, :], 0.0).astype(BF)
            for k in range(5)
        ],
        axis=1,
    )
    copies[3].wait()
    pre = dot(taps, second_mat[...])
    act, slope = gelu_both(pre)
    slope_2_ref[0:144, :] = slope
    far = right_ref[...].astype(F32)
    far = [
        jnp.concatenate([far[row : row + 1], far[row + 1 : row + 2]], axis=1)
        for row in range(24, 42, 2)
    ]
    slope_2_ref[144:160, :] = jnp.concatenate(far + [jnp.zeros((7, 1024), F32)], axis=0)
    sent.append(send(3))
    wait_for(copies[4:])

    same = lax.broadcasted_iota(jnp.int32, (16, 16), 0) == lax.broadcasted_iota(
        jnp.int32, (16, 16), 1
    )

    def column(row):
        return jnp.sum(jnp.where(same, row, 0.0), axis=1, keepdims=True)

    donor, accept = (donor_ref[...] - 6) & 2047, (accept_ref[...] - 6) & 2047
    live = lax.broadcasted_iota(jnp.int32, (1, 16), 1) < live_ref[0]
    weight = column(jnp.where(live, cot_ref[...], 0.0) * (1024 ** -0.5))
    lane = lax.broadcasted_iota(jnp.int32, (16, 128), 1)
    info = jnp.zeros((16, 128), F32)
    for place, value in enumerate(
        [
            column((donor >> 6).astype(F32)),
            column((donor & 63).astype(F32)),
            column((accept >> 6).astype(F32)),
            column((accept & 63).astype(F32)),
            weight,
            weight - rounded(weight),
        ]
    ):
        info = jnp.where(lane == place, value, info)
    info = info.astype(BF)
    left = half_lanes(64)
    for pair in range(8):
        top = act[8:72, 128 * pair : 128 * pair + 128]
        low = act[72:136, 128 * pair : 128 * pair + 128]
        mess_ref[2 * pair, 0:64, :] = jnp.where(left, top, swap(low)).astype(BF)
        mess_ref[2 * pair + 1, 0:64, :] = jnp.where(left, swap(top), low).astype(BF)
    for target in range(16):
        mess_ref[target, 64:80, :] = info
    sent.append(send(0))
    wait_for(sent)


def forward_part(seq_index, live, inputs, right, donor, accept, cot, w_first, w_second):
    return pl.pallas_call(
        forward_kernel,
        out_shape=[
            jax.ShapeDtypeStruct((16, 80, 128), BF),
            jax.ShapeDtypeStruct((384, 512), BF),
            jax.ShapeDtypeStruct((288, 512), F32),
            jax.ShapeDtypeStruct((160, 1024), F32),
        ],
        in_specs=[SMEM, SMEM, HBM, ANY] + [HBM] * 5,
        out_specs=[HBM] * 4,
        scratch_shapes=[
            pltpu.VMEM((256, 512), BF),
            pltpu.VMEM((48, 512), BF),
            pltpu.VMEM((2560, 512), BF),
            pltpu.VMEM((2560, 1024), BF),
            pltpu.VMEM((1, 16), jnp.int32),
            pltpu.VMEM((1, 16), jnp.int32),
            pltpu.VMEM((1, 16), F32),
            pltpu.VMEM((16, 80, 128), BF),
            pltpu.VMEM((384, 512), BF),
            pltpu.VMEM((288, 512), F32),
            pltpu.VMEM((160, 1024), F32),
            pltpu.VMEM((320, 512), F32),
            pltpu.VMEM((1152, 128), F32),
            pltpu.VMEM((160, 512), F32),
            pltpu.SemaphoreType.DMA((7,)),
            pltpu.SemaphoreType.DMA((4,)),
        ],
        compiler_params=pltpu.CompilerParams(vmem_limit_bytes=56 * MEBI),
        cost_estimate=pl.CostEstimate(
            flops=15 * 10**8, bytes_accessed=10 * 10**6, transcendentals=3 * 10**5
        ),
        name="forward",
    )(
        seq_index, live, inputs, right,
        w_first.reshape(2560, 512), w_second.reshape(2560, 1024), donor, accept, cot,
    )


def pair_kernel(
    seq_ref, got_ref, head_hbm, sent_hbm, term_hbm, head_ref, sent_ref, term_ref, sems
):
    head_copy = started([(head_hbm, head_ref)], sems)
    seq_index = seq_ref[0]
    flat = jnp.concatenate([got_ref[i] for i in range(16)], axis=0)
    info = jnp.concatenate([got_ref[i, 64:80, :].astype(F32) for i in range(16)], axis=0)
    donor = (info[:, 0:1] * 64.0 + info[:, 1:2]).astype(jnp.int32)
    accept = (info[:, 2:3] * 64.0 + info[:, 3:4]).astype(jnp.int32)
    weight = info[:, 4:5] + info[:, 5:6]
    spots = jnp.concatenate([donor, accept], axis=0)
    row_of = (spots >> 7) * 80 + (spots & 63)
    pick = (row_of == lax.broadcasted_iota(jnp.int32, (512, 1280), 1)).astype(F32).astype(BF)
    rows = dot(pick, flat)
    rows = jnp.where((spots & 127) < 64, rows, swap(rows))[:, :64]
    donor_rows, accept_rows = rows[:256], rows[256:]
    both = donor_rows * accept_rows
    wait_for(head_copy)
    head_row = head_ref[pl.ds(seq_index // 2, 1), :]
    head_row = jnp.where(seq_index % 2 == 0, head_row, swap(head_row))[:, :64]
    partial = jnp.sum(both * head_row, axis=1, keepdims=True)
    term = jnp.sum(weight * both, axis=0, keepdims=True)
    term_high = rounded(term)
    term_ref[...] = jnp.concatenate([term_high, term - term_high], axis=1)
    copies = [pltpu.make_async_copy(term_ref, term_hbm, sems.at[4])]
    copies[0].start()
    scaled = weight * head_row
    grads = jnp.concatenate([scaled * accept_rows, scaled * donor_rows], axis=0)
    blank = jnp.zeros((512, 64), F32)
    grads = jnp.concatenate(
        [
            jnp.concatenate([grads, blank], axis=1),
            jnp.concatenate([blank, grads], axis=1),
        ],
        axis=0,
    ).astype(BF)
    lane = lax.broadcasted_iota(jnp.int32, (256, 128), 1)
    turned = jnp.where(
        lane == 0,
        donor.astype(F32),
        jnp.where(lane == 1, accept.astype(F32), jnp.where(lane == 2, partial, 0.0)),
    ).T
    spot_row = jnp.concatenate([turned[0:1, :], turned[1:2, :]], axis=1).astype(jnp.int32)
    high = rounded(turned[2:3, :])
    rest = turned[2:3, :] - high
    extra = jnp.concatenate(
        [
            jnp.zeros((4, 128), F32),
            high[:, :128],
            high[:, 128:],
            rest[:, :128],
            rest[:, 128:],
            jnp.zeros((8, 128), F32),
        ],
        axis=0,
    )
    index = lax.broadcasted_iota(jnp.int32, (80, 1), 0)
    low_row = jnp.where(index < 64, index, index - 67)
    high_row = index + 64
    for group in range(4):
        picks = []
        for target in range(4 * group, 4 * group + 4):
            base = 128 * target
            low_pick = jnp.where(index < 67, (low_row + base) & 2047, -1) == spot_row
            high_pick = jnp.where(index < 67, (high_row + base) & 2047, -1) == spot_row
            picks.append(jnp.concatenate([low_pick.astype(F32), high_pick.astype(F32)], axis=1))
        pieces = dot(jnp.concatenate(picks, axis=0).astype(BF), grads)
        for place in range(4):
            target = 4 * group + place
            piece = pieces[80 * place : 80 * place + 80]
            sent_ref[target, 0:64, :] = piece[0:64].astype(BF)
            sent_ref[target, 64:80, :] = (piece[64:80] + extra).astype(BF)
        part = pl.ds(4 * group, 4)
        copies.append(pltpu.make_async_copy(sent_ref.at[part], sent_hbm.at[part], sems.at[group]))
        copies[-1].start()
    wait_for(copies)


def pair_part(seq_index, got, head_vec):
    return pl.pallas_call(
        pair_kernel,
        out_shape=[
            jax.ShapeDtypeStruct((16, 80, 128), BF),
            jax.ShapeDtypeStruct((1, 128), F32),
        ],
        in_specs=[SMEM, VMEM, HBM],
        out_specs=[HBM] * 2,
        scratch_shapes=[
            pltpu.VMEM((8, 128), F32),
            pltpu.VMEM((16, 80, 128), BF),
            pltpu.VMEM((1, 128), F32),
            pltpu.SemaphoreType.DMA((5,)),
        ],
        compiler_params=pltpu.CompilerParams(vmem_limit_bytes=52 * MEBI),
        cost_estimate=pl.CostEstimate(
            flops=5 * 10**8, bytes_accessed=10**6, transcendentals=0
        ),
        name="pairs",
    )(seq_index, got, head_vec.reshape(8, 128))


def backward_kernel(seq_ref, live_ref, back_ref, *refs):
    sources, second_hbm, outs = refs[:3], refs[3], refs[4:8]
    held, second_mat, staged = refs[8:11], refs[11], refs[12:16]
    track_ref, slope_2_ref, slope_1_ref = held
    mess_ref, grad_1_ref, grad_y_ref, scores_ref = staged
    wide, grad_y, grad_1, sems, out_sems = refs[16:]
    seq_index = seq_ref[0]
    parts = [pl.ds(512 * k, 512) for k in range(5)]
    copies = started(
        list(zip(sources, held)) + [(second_hbm.at[part], second_mat.at[part]) for part in parts],
        sems,
    )

    def send(place, part, sem):
        copy = pltpu.make_async_copy(part(staged[place]), part(outs[place]), out_sems.at[sem])
        copy.start()
        return copy

    def all_of(ref):
        return ref

    left = half_lanes(64)
    edge = half_lanes(16)
    wide[0:16, :] = jnp.zeros((16, 1024), F32)
    wide[144:160, :] = jnp.zeros((16, 1024), F32)
    for pair in range(8):
        lanes = slice(128 * pair, 128 * pair + 128)
        one = back_ref[2 * pair, 0:64, :].astype(F32)
        two = back_ref[2 * pair + 1, 0:64, :].astype(F32)
        wide[16:80, lanes] = jnp.where(left, one, swap(two))
        wide[80:144, lanes] = jnp.where(left, swap(one), two)
        one = back_ref[2 * pair, 64:80, :].astype(F32)
        two = back_ref[2 * pair + 1, 64:80, :].astype(F32)
        wide[13:16, lanes] = jnp.where(edge, one, swap(two))[0:3]
        wide[144:147, lanes] = jnp.where(edge, swap(one), two)[0:3]
    copies[0].wait()
    wide[13:138, :] = wide[13:138, :] + track_ref[...].astype(F32)[3:128]
    copies[1].wait()
    wide[138:147, :] = wide[138:147, :] + slope_2_ref[144:153, :]
    wide[8:152, :] = wide[8:152, :] * slope_2_ref[0:144, :]
    for target in range(8):
        mess_ref[target, 144:288, :] = wide[8:152, 128 * target : 128 * target + 128].astype(BF)
    sent = [send(0, lambda ref: ref.at[:, pl.ds(144, 144)], 0)]
    pooled = jnp.zeros((144, 512), F32)
    for k in range(5):
        copies[3 + k].wait()
        pooled = pooled + dot(
            jnp.where(within(144, 130, 2 - k, seq_index), wide[10 - k : 154 - k, :], 0.0).astype(BF),
            second_mat[512 * k : 512 * k + 512, :],
            ((1,), (1,)),
        )
    pooled = 0.5 * pooled
    copies[2].wait()
    for tile in range(4):
        lanes = slice(128 * tile, 128 * tile + 128)
        grad_y[pl.ds(288 * tile, 144, 2), :] = pooled[:, lanes]
        grad_y[pl.ds(288 * tile + 1, 144, 2), :] = pooled[:, lanes]
        value = grad_y[288 * tile : 288 * tile + 288, :]
        grad_y_ref[:, lanes] = value[16:272]
        value = value * slope_1_ref[:, lanes]
        grad_1[:, lanes] = value
        grad_1_ref[:, lanes] = value.astype(BF)
    sent += [send(1, all_of, 1), send(2, all_of, 2)]
    left = half_lanes(144)
    for pair in range(4):
        lanes = slice(128 * pair, 128 * pair + 128)
        one = grad_1[8:152, lanes]
        two = grad_1[136:280, lanes]
        mess_ref[2 * pair, 0:144, :] = jnp.where(left, one, swap(two)).astype(BF)
        mess_ref[2 * pair + 1, 0:144, :] = jnp.where(left, swap(one), two).astype(BF)
    sent.append(send(0, lambda ref: ref.at[:, pl.ds(0, 144)], 3))
    total = jnp.zeros((16, 128), F32)
    for source in range(16):
        total = total + back_ref[source, 64:80, :].astype(F32)
    row = jnp.where(seq_index < 8, total[4:5] + total[6:7], total[5:6] + total[7:8])
    row = pltpu.roll(row, 128 - 16 * (seq_index % 8), 1)[:, :16]
    live = lax.broadcasted_iota(jnp.int32, (1, 16), 1) < live_ref[0]
    scores_ref[...] = jnp.where(live, row * (1024 ** -0.5), 0.0)
    sent.append(send(3, all_of, 4))
    wait_for(sent)


def backward_part(seq_cell, live, back, track, slope_first, slope_second, w_second):
    return pl.pallas_call(
        backward_kernel,
        out_shape=[
            jax.ShapeDtypeStruct((8, 288, 128), BF),
            jax.ShapeDtypeStruct((288, 512), BF),
            jax.ShapeDtypeStruct((256, 512), F32),
            jax.ShapeDtypeStruct((1, 16), F32),
        ],
        in_specs=[SMEM] * 2 + [VMEM] + [HBM] * 4,
        out_specs=[HBM] * 4,
        scratch_shapes=[
            pltpu.VMEM((128, 1024), BF),
            pltpu.VMEM((160, 1024), F32),
            pltpu.VMEM((288, 512), F32),
            pltpu.VMEM((2560, 1024), BF),
            pltpu.VMEM((8, 288, 128), BF),
            pltpu.VMEM((288, 512), BF),
            pltpu.VMEM((256, 512), F32),
            pltpu.VMEM((1, 16), F32),
            pltpu.VMEM((160, 1024), F32),
            pltpu.VMEM((1152, 128), F32),
            pltpu.VMEM((288, 512), F32),
            pltpu.SemaphoreType.DMA((8,)),
            pltpu.SemaphoreType.DMA((5,)),
        ],
        compiler_params=pltpu.CompilerParams(vmem_limit_bytes=52 * MEBI),
        cost_estimate=pl.CostEstimate(
            flops=8 * 10**8, bytes_accessed=10 * 10**6, transcendentals=0
        ),
        name="backward",
    )(
        seq_cell, live, back, track, slope_second, slope_first,
        w_second.reshape(2560, 1024),
    )


def input_kernel(seq_ref, *refs):
    sources, (out_ref, tail_ref), held, (grad_1, sems) = refs[:3], refs[3:5], refs[5:8], refs[8:]
    grad_ref, grad_y_ref, first_mat = held
    copies = started(list(zip(sources, held)), sems)
    copies[0].wait()
    grad_1[...] = grad_ref[...].astype(F32)
    wait_for(copies[1:])
    total = grad_y_ref[...]
    for k in range(5):
        rows = jnp.where(within(256, 244, 2 - k, seq_ref[0]), grad_1[18 - k : 274 - k, :], 0.0)
        total = total + dot(
            rows.astype(BF), first_mat[512 * k : 512 * k + 512, :], ((1,), (1,))
        )
    out_ref[...] = total.astype(BF)
    tail_ref[...] = total[240:256].astype(BF)


def input_part(seq_cell, grad_y, grad_first_pre, w_first):
    return pl.pallas_call(
        input_kernel,
        out_shape=[
            jax.ShapeDtypeStruct((256, 512), BF),
            jax.ShapeDtypeStruct((16, 512), BF),
        ],
        in_specs=[SMEM] + [HBM] * 3,
        out_specs=[VMEM] * 2,
        scratch_shapes=[
            pltpu.VMEM((288, 512), BF),
            pltpu.VMEM((256, 512), F32),
            pltpu.VMEM((2560, 512), BF),
            pltpu.VMEM((288, 512), F32),
            pltpu.SemaphoreType.DMA((3,)),
        ],
        compiler_params=pltpu.CompilerParams(vmem_limit_bytes=52 * MEBI),
        cost_estimate=pl.CostEstimate(
            flops=7 * 10**8, bytes_accessed=4 * 10**6, transcendentals=0
        ),
        name="inputs",
    )(seq_cell, grad_first_pre, grad_y, w_first.reshape(2560, 512))


def term_kernel(dp_ref, seq_ref, *refs):
    sources, out_hbm, held, out_ref = refs[:10], refs[10], refs[11:21], refs[21]
    part_scr, wide_1, wide_2, sum_1, sum_2, mess, sems, out_sems = refs[22:]
    got_ref, head_ref, columns = held[0], held[1], held[2:]
    copies = started(list(zip(sources, held)), sems)
    copies[0].wait()
    left = half_lanes(128)
    fit_1 = [half_lanes(16) | within(16, 4, 2 - k, seq_ref[0]) for k in range(5)]
    fit_2 = [within(16, 10, 2 - k, seq_ref[0]) for k in range(5)]
    for step in range(8):
        part_scr[...] = got_ref[dp_ref[0] ^ step].astype(F32)
        taps = []
        for k in range(5):
            ends = jnp.where(fit_1[k], part_scr[122 - k : 138 - k, :], 0.0)
            taps.append(jnp.concatenate([part_scr[10 - k : 122 - k, :], ends], axis=0))
            lanes = slice(128 * k, 128 * k + 128)
            wide_2[128 * step : 128 * step + 112, lanes] = part_scr[154 - k : 266 - k, :].astype(BF)
            wide_2[128 * step + 112 : 128 * step + 128, lanes] = jnp.where(
                fit_2[k], part_scr[266 - k : 282 - k, :], 0.0
            ).astype(BF)
        top = [
            jnp.where(left, taps[0], swap(taps[1])),
            jnp.where(left, taps[2], swap(taps[3])),
            taps[4],
        ]
        low = [
            jnp.where(left, swap(taps[0]), taps[1]),
            jnp.where(left, swap(taps[2]), taps[3]),
            swap(taps[4]),
        ]
        for place in range(3):
            lanes = slice(128 * place, 128 * place + 128)
            wide_1[256 * step : 256 * step + 128, lanes] = top[place].astype(BF)
            wide_1[256 * step + 128 : 256 * step + 256, lanes] = low[place].astype(BF)
    wait_for(copies[1:])
    lefts = jnp.concatenate([ref[:, 0:256] for ref in columns], axis=1)
    first = dot(lefts, wide_1[...])
    lefts = jnp.concatenate([ref[:, 256:384] for ref in columns], axis=1)
    second = dot(lefts, wide_2[...])
    left = half_lanes(512)
    for k in range(5):
        sum_2[512 * k : 512 * k + 512, :] = second[:, 128 * k : 128 * k + 128]
        tile = first[:, 128 * (k // 2) : 128 * (k // 2) + 128]
        turned = swap(tile)
        sum_1[512 * k : 512 * k + 512, :] = (
            jnp.where(left, tile, turned) if k % 2 == 0 else jnp.where(left, turned, tile)
        )
    left = half_lanes(10)
    head = jnp.concatenate([head_ref[...], jnp.zeros((1, 128), F32)], axis=0)
    sent = []
    for owner in range(128):
        row = 20 * owner
        slot = owner % 4
        mess[slot, 0:20, :] = sum_2[row : row + 20, :]
        mess[slot, 20:30, :] = jnp.where(
            left, sum_1[row : row + 10, :], sum_1[row + 10 : row + 20, :]
        )
        if owner < 4:
            mess[slot, 30:32, :] = head
        out_ref[owner] = mess[slot].astype(BF)
        if owner % 32 == 31:
            part = pl.ds(owner - 31, 32)
            sent.append(
                pltpu.make_async_copy(out_ref.at[part], out_hbm.at[part], out_sems.at[owner // 32])
            )
            sent[-1].start()
    wait_for(sent)


def term_part(columns, got, head_row, dp_index, seq_cell):
    return pl.pallas_call(
        term_kernel,
        out_shape=jax.ShapeDtypeStruct((128, 32, 128), BF),
        in_specs=[SMEM] * 2 + [ANY] * 2 + [HBM] * 8,
        out_specs=HBM,
        scratch_shapes=[
            pltpu.VMEM((8, 288, 128), BF),
            pltpu.VMEM((1, 128), F32),
        ]
        + [pltpu.VMEM((512, 384), BF)] * 8
        + [
            pltpu.VMEM((128, 32, 128), BF),
            pltpu.VMEM((288, 128), F32),
            pltpu.VMEM((2048, 384), BF),
            pltpu.VMEM((1024, 640), BF),
            pltpu.VMEM((2560, 128), F32),
            pltpu.VMEM((2560, 128), F32),
            pltpu.VMEM((4, 32, 128), F32),
            pltpu.SemaphoreType.DMA((10,)),
            pltpu.SemaphoreType.DMA((4,)),
        ],
        compiler_params=pltpu.CompilerParams(vmem_limit_bytes=52 * MEBI),
        cost_estimate=pl.CostEstimate(flops=3 * 10**9, bytes_accessed=5 * 10**6, transcendentals=0),
        name="terms",
    )(jnp.reshape(dp_index, (1,)), seq_cell, got, head_row, *columns)


def final_kernel(final_ref, first_ref, second_ref, head_ref):
    left = half_lanes(10)
    for pair in range(4):
        sums = []
        for block in (2 * pair, 2 * pair + 1):
            total = final_ref[16 * block].astype(F32)
            for source in range(1, 16):
                total = total + final_ref[16 * block + source].astype(F32)
            second_ref[:, 128 * block : 128 * block + 128] = total[0:20]
            sums.append(total[20:30])
        one, two = sums
        lanes = slice(128 * pair, 128 * pair + 128)
        first_ref[0:10, lanes] = jnp.where(left, one, swap(two))
        first_ref[10:20, lanes] = jnp.where(left, swap(one), two)
    left = half_lanes(16)
    for pair in range(8):
        sums = []
        for source in (2 * pair, 2 * pair + 1):
            total = final_ref[source, 16:32, :].astype(F32)
            for block in range(1, 8):
                total = total + final_ref[16 * block + source, 16:32, :].astype(F32)
            sums.append(total + swap(total))
        head_ref[pair : pair + 1, :] = jnp.where(left, sums[0], sums[1])[14:15]


def final_part(final):
    return pl.pallas_call(
        final_kernel,
        out_shape=[
            jax.ShapeDtypeStruct((20, 512), F32),
            jax.ShapeDtypeStruct((20, 1024), F32),
            jax.ShapeDtypeStruct((8, 128), F32),
        ],
        in_specs=[VMEM],
        out_specs=[VMEM] * 3,
        compiler_params=pltpu.CompilerParams(vmem_limit_bytes=50 * MEBI),
        name="final",
    )(final)


def per_device(
    seq_in, w_first, w_second, head_vec, track_cot, donor_pos, acceptor_pos, pair_cot, live_pairs
):
    seq_index = lax.axis_index("seq")
    seq_cell = jnp.reshape(seq_index, (1,))
    dp_index = lax.axis_index("dp")
    inputs, track = seq_in[0], track_cot[0]
    right = edges(inputs, track, 16)
    message, mine, slope_first, slope_second = forward_part(
        seq_cell, live_pairs[0], inputs, right, donor_pos, acceptor_pos, pair_cot,
        w_first, w_second,
    )
    got = lax.all_to_all(message, "seq", 0, 0, tiled=True)

    mine = mine.T

    def passed(value, step):
        return lax.ppermute(value, "dp", [(i, i ^ step) for i in range(8)])

    own = [mine] + [passed(mine, step) for step in (2, 4, 6)]
    sent, head_row = pair_part(seq_cell, got, head_vec)
    back = lax.all_to_all(sent, "seq", 0, 0, tiled=True)
    back, *own = lax.optimization_barrier((back, *own))
    message, grad_1, grad_y, scores = backward_part(
        seq_cell, live_pairs[0], back, track, slope_first, slope_second, w_second
    )
    other = [passed(value, 1) for value in own]
    columns = [(own, other)[step % 2][step // 2] for step in range(8)]
    grads = lax.all_to_all(message, "dp", 0, 0, tiled=True)
    grad_input, tail = input_part(seq_cell, grad_y, grad_1, w_first)
    before = lax.ppermute(tail, "seq", [(i, (i + 1) % 16) for i in range(16)])
    terms = term_part(columns, grads, head_row, dp_index, seq_cell)
    terms, before = lax.optimization_barrier((terms, before))
    grad_input = jnp.concatenate([before[4:], grad_input[:244]], axis=0)
    final = lax.all_to_all(terms, ("dp", "seq"), 0, 0, tiled=True)
    out_first, out_second, grad_head = final_part(final)
    return (scores, out_first, out_second, grad_input[None], grad_head.reshape(1024))


def solution(mesh):
    in_specs = (
        P("dp", "seq", None),
        P(),
        P(),
        P(),
        P("dp", "seq", None),
        P("dp", "seq"),
        P("dp", "seq"),
        P("dp", "seq"),
        P("dp", "seq"),
    )
    out_specs = (
        P("dp", "seq"),
        P(("dp", "seq"), None),
        P(("dp", "seq"), None),
        P("dp", "seq", None),
        P(),
    )
    return jax.shard_map(
        per_device, mesh=mesh, in_specs=in_specs, out_specs=out_specs, check_vma=False
    )
```

profile of v0, /device:TPU:1, one launch (start us, length us, event | category | flops | bytes accessed | tf_op | source)
XLA Modules:
  0.0 99.8 jit_solution(7740868643712058888)
XLA Ops:
  0.6 1.4 %edges.1 = bf16[48,512]{1,0:T(8,128)(2,1)} custom-call(bf16[256,512]{1,0:T(8,128)(2,1)} %bitcast.26, bf16[128,1024]{1,0:T(8,128)(2,1)} %bitcast.14), custom_call_target="tpu_custom_call" | custom-call | tf_op jit(solution)/shard_map/edges/pallas_call | solution.py:83
  2.1 5.8 %collective-permute-start = (bf16[48,512]{1,0:T(8,128)(2,1)}, bf16[48,512]{1,0:T(8,128)(2,1)S(1)}, u32[]{:S(2)}, u32[]{:S(2)}) collective-permute-start(bf16[48,512]{1,0:T(8,128)(2,1)} %edges.1), channel_id=1, source_target_pairs={{0,15},{1,0},{2,1},{3,2},{4,3},{5,4},{6,5},{7,6},{8,7},{9,8},{10,9... | collective-permute-start | bytes 147464 | tf_op jit(solution)/shard_map/ppermute | solution.py:97
  8.6 0.8 collective-permute-done.refs_1_
  9.4 0.6 copy-done.2
  10.0 5.8 %forward.1 = (bf16[16,80,128]{2,1,0:T(8,128)(2,1)}, bf16[384,512]{1,0:T(8,128)(2,1)}, f32[288,512]{1,0:T(8,128)}, f32[160,1024]{1,0:T(8,128)}) custom-call(s32[1]{0:T(128)} %bitcast.seq_ref, s32[1]{0:T(128)} %bitcast.12.live_ref, bf16[256,512]{1,0:T(8,128)(2,1)} %bitcast.27, bf16[48,512]{1,0:T(8,128)(2,1)} %copy-done.2, bf16[2560,512]{1,0:T(8,128)(2,1)} %bitcast.24, ...), custom_call_target="tpu_custom_call" | custom-call | flops 1500000000 | bytes 10000000 | tf_op jit(solution)/shard_map/forward/pallas_call | solution.py:200
  15.8 6.4 %all-to-all-start = ((bf16[16,80,128]{2,1,0:T(8,128)(2,1)}), bf16[16,80,128]{2,1,0:T(8,128)(2,1)S(1)}, u32[]{:S(2)}, u32[]{:S(2)}) async-start(bf16[16,80,128]{2,1,0:T(8,128)(2,1)} %get-tuple-element.27), calls=%async_computation | async-start | bytes 655360 | tf_op jit(solution)/shard_map/all_to_all | solution.py:649
  22.2 1.2 %copy.14 = bf16[384,512]{0,1:T(8,128)(2,1)S(1)} copy(bf16[384,512]{1,0:T(8,128)(2,1)} %get-tuple-element.29) | data formatting | bytes 786432 | tf_op jit(solution)/shard_map/forward/pallas_call | solution.py:200
  23.4 3.8 %collective-permute-start.3 = (bf16[512,384]{1,0:T(8,128)(2,1)S(1)}, bf16[512,384]{1,0:T(8,128)(2,1)S(1)}, u32[]{:S(2)}, u32[]{:S(2)}) collective-permute-start(bf16[512,384]{1,0:T(8,128)(2,1)S(1)} %bitcast.16), channel_id=1, source_target_pairs={{0,96},{16,112},{32,64},{48,80},{64,32},{80,48},{96,0},{112,16},{1... | collective-permute-start | bytes 1179656 | tf_op jit(solution)/shard_map/ppermute | solution.py:654
  27.2 0.0 collective-permute-start.2
  27.2 0.7 collective-permute-start.1
  27.9 2.2 %all-to-all-done.got_ref = bf16[16,80,128]{2,1,0:T(8,128)(2,1)S(1)} async-done(((bf16[16,80,128]{2,1,0:T(8,128)(2,1)}), bf16[16,80,128]{2,1,0:T(8,128)(2,1)S(1)}, u32[]{:S(2)}, u32[]{:S(2)}) %all-to-all-start) | async-done | bytes 327712 | tf_op jit(solution)/shard_map/all_to_all | solution.py:649
  30.1 3.4 %pairs.1 = (bf16[16,80,128]{2,1,0:T(8,128)(2,1)}, f32[1,128]{1,0:T(1,128)S(1)}) custom-call(s32[1]{0:T(128)} %bitcast.seq_ref, bf16[16,80,128]{2,1,0:T(8,128)(2,1)S(1)} %all-to-all-done.got_ref, f32[8,128]{1,0:T(8,128)S(1)} %bitcast.21), custom_call_target="tpu_custom_call" | custom-call | flops 500000000 | bytes 1000000 | tf_op jit(solution)/shard_map/pairs/pallas_call | solution.py:318
  33.6 4.5 %all-to-all-start.1 = ((bf16[16,80,128]{2,1,0:T(8,128)(2,1)}), bf16[16,80,128]{2,1,0:T(8,128)(2,1)S(1)}, u32[]{:S(2)}, u32[]{:S(2)}) async-start(bf16[16,80,128]{2,1,0:T(8,128)(2,1)} %get-tuple-element.28), calls=%async_computation.1 | async-start | bytes 655360 | tf_op jit(solution)/shard_map/all_to_all | solution.py:658
  38.0 6.0 %collective-permute-done.3.refs_8_ = bf16[512,384]{1,0:T(8,128)(2,1)S(1)} collective-permute-done((bf16[512,384]{1,0:T(8,128)(2,1)S(1)}, bf16[512,384]{1,0:T(8,128)(2,1)S(1)}, u32[]{:S(2)}, u32[]{:S(2)}) %collective-permute-start.3) | collective-permute-done | bytes 393248 | tf_op jit(solution)/shard_map/ppermute | solution.py:654
  44.0 0.0 collective-permute-done.2.refs_6_
  44.0 0.0 collective-permute-done.1.refs_4_
  44.1 1.9 %all-to-all-done.1.back_ref = bf16[16,80,128]{2,1,0:T(8,128)(2,1)S(1)} async-done(((bf16[16,80,128]{2,1,0:T(8,128)(2,1)}), bf16[16,80,128]{2,1,0:T(8,128)(2,1)S(1)}, u32[]{:S(2)}, u32[]{:S(2)}) %all-to-all-start.1) | async-done | bytes 327712 | tf_op jit(solution)/shard_map/all_to_all | solution.py:658
  45.9 5.3 %backward.1 = (bf16[8,288,128]{2,1,0:T(8,128)(2,1)}, bf16[288,512]{1,0:T(8,128)(2,1)S(1)}, f32[256,512]{1,0:T(8,128)S(1)}, f32[1,16]{1,0:T(1,128)}) custom-call(s32[1]{0:T(128)} %bitcast.seq_ref, s32[1]{0:T(128)} %bitcast.13.live_ref, bf16[16,80,128]{2,1,0:T(8,128)(2,1)S(1)} %all-to-all-done.1.back_ref, bf16[128,1024]{1,0:T(8,128)(2,1)S(1)} %bitcast.15, ...), custom_call_target="tpu_custom_call" | custom-call | flops 800000000 | bytes 10000000 | tf_op jit(solution)/shard_map/backward/pallas_call | solution.py:423
  51.2 8.8 %all-to-all-start.2 = ((bf16[8,288,128]{2,1,0:T(8,128)(2,1)}), bf16[8,288,128]{2,1,0:T(8,128)(2,1)}, u32[]{:S(2)}, u32[]{:S(2)}) async-start(bf16[8,288,128]{2,1,0:T(8,128)(2,1)} %get-tuple-element.34), calls=%async_computation.2 | async-start | bytes 1179648 | tf_op jit(solution)/shard_map/all_to_all | solution.py:665
  60.0 0.0 collective-permute-start.4
  60.0 0.5 collective-permute-start.5
  60.5 0.0 collective-permute-start.6
  60.5 0.5 collective-permute-start.7
  61.0 2.7 %inputs.1 = (bf16[256,512]{1,0:T(8,128)(2,1)S(1)}, bf16[16,512]{1,0:T(8,128)(2,1)S(1)}) custom-call(s32[1]{0:T(128)} %bitcast.seq_ref, bf16[288,512]{1,0:T(8,128)(2,1)S(1)} %get-tuple-element.40.refs_0_, f32[256,512]{1,0:T(8,128)S(1)} %get-tuple-element.41.refs_1_, bf16[2560,512]{1,0:T(8,128)(2,1)} %bitcast.25), custom_call_target="tpu_custom_call" | custom-call | flops 700000000 | bytes 4000000 | tf_op jit(solution)/shard_map/inputs/pallas_call | solution.py:477
  63.8 0.5 collective-permute-start.8
  64.3 0.0 collective-permute-done.5.refs_5_
  64.3 6.0 %all-to-all-done.2.refs_0_ = bf16[8,288,128]{2,1,0:T(8,128)(2,1)} async-done(((bf16[8,288,128]{2,1,0:T(8,128)(2,1)}), bf16[8,288,128]{2,1,0:T(8,128)(2,1)}, u32[]{:S(2)}, u32[]{:S(2)}) %all-to-all-start.2) | async-done | bytes 589856 | tf_op jit(solution)/shard_map/all_to_all | solution.py:665
  70.3 5.4 %terms.1 = bf16[128,32,128]{2,1,0:T(8,128)(2,1)} custom-call(s32[1]{0:T(128)} %bitcast.8.dp_ref, s32[1]{0:T(128)} %bitcast.seq_ref, bf16[8,288,128]{2,1,0:T(8,128)(2,1)} %all-to-all-done.2.refs_0_, f32[1,128]{1,0:T(1,128)S(1)} %get-tuple-element.35.refs_1_, bf16[512,384]{1,0:T(8,128)(2,1)S(1)} %bitcast.20, ...), custom_call_target="tpu_custom_call" | custom-call | flops 3000000000 | bytes 5000000 | tf_op jit(solution)/shard_map/terms/pallas_call | solution.py:570
  75.7 4.3 %all-to-all-start.3 = ((bf16[128,32,128]{2,1,0:T(8,128)(2,1)}), bf16[128,32,128]{2,1,0:T(8,128)(2,1)S(1)}, u32[]{:S(2)}, u32[]{:S(2)}) async-start(bf16[128,32,128]{2,1,0:T(8,128)(2,1)} %terms.1), calls=%async_computation.3 | async-start | bytes 2097152 | tf_op jit(solution)/shard_map/all_to_all | solution.py:671
  80.0 0.8 maximum_bitcast_fusion
  80.8 18.1 %all-to-all-done.3.final_ref = bf16[128,32,128]{2,1,0:T(8,128)(2,1)S(1)} async-done(((bf16[128,32,128]{2,1,0:T(8,128)(2,1)}), bf16[128,32,128]{2,1,0:T(8,128)(2,1)S(1)}, u32[]{:S(2)}, u32[]{:S(2)}) %all-to-all-start.3) | async-done | bytes 1048608 | tf_op jit(solution)/shard_map/all_to_all | solution.py:671
  98.9 0.8 final.1
  (13 shorter events, 0.1 us)
Async XLA Ops:
  0.6 29.5 %copy-start.1 = (f32[1024]{0:T(1024)S(1)}, f32[1024]{0:T(1024)}, u32[]{:S(2)}) copy-start(f32[1024]{0:T(1024)} %param.12) | copy-start | bytes 12292
  2.1 7.3 %collective-permute-start = (bf16[48,512]{1,0:T(8,128)(2,1)}, bf16[48,512]{1,0:T(8,128)(2,1)S(1)}, u32[]{:S(2)}, u32[]{:S(2)}) collective-permute-start(bf16[48,512]{1,0:T(8,128)(2,1)} %edges.1), channel_id=1, source_target_pairs={{0,15},{1,0},{2,1},{3,2},{4,3},{5,4},{6,5},{7,6},{8,7},{9,8},{10,9... | collective-permute-start | bytes 147464 | tf_op jit(solution)/shard_map/ppermute | solution.py:97
  9.4 0.6 copy-start.2
  10.0 35.9 %copy-start = (bf16[1,128,1024]{2,1,0:T(8,128)(2,1)S(1)}, bf16[1,128,1024]{2,1,0:T(8,128)(2,1)}, u32[]{:S(2)}) copy-start(bf16[1,128,1024]{2,1,0:T(8,128)(2,1)} %param.13) | copy-start | bytes 786436
  15.8 14.3 %all-to-all-start = ((bf16[16,80,128]{2,1,0:T(8,128)(2,1)}), bf16[16,80,128]{2,1,0:T(8,128)(2,1)S(1)}, u32[]{:S(2)}, u32[]{:S(2)}) async-start(bf16[16,80,128]{2,1,0:T(8,128)(2,1)} %get-tuple-element.27), calls=%async_computation | async-start | bytes 655360 | tf_op jit(solution)/shard_map/all_to_all | solution.py:649
  23.4 20.6 %collective-permute-start.3 = (bf16[512,384]{1,0:T(8,128)(2,1)S(1)}, bf16[512,384]{1,0:T(8,128)(2,1)S(1)}, u32[]{:S(2)}, u32[]{:S(2)}) collective-permute-start(bf16[512,384]{1,0:T(8,128)(2,1)S(1)} %bitcast.16), channel_id=1, source_target_pairs={{0,96},{16,112},{32,64},{48,80},{64,32},{80,48},{96,0},{112,16},{1... | collective-permute-start | bytes 1179656 | tf_op jit(solution)/shard_map/ppermute | solution.py:654
  27.2 16.8 %collective-permute-start.2 = (bf16[512,384]{1,0:T(8,128)(2,1)S(1)}, bf16[512,384]{1,0:T(8,128)(2,1)S(1)}, u32[]{:S(2)}, u32[]{:S(2)}) collective-permute-start(bf16[512,384]{1,0:T(8,128)(2,1)S(1)} %bitcast.17), channel_id=1, source_target_pairs={{0,64},{16,80},{32,96},{48,112},{64,0},{80,16},{96,32},{112,48},{1... | collective-permute-start | bytes 1179656 | tf_op jit(solution)/shard_map/ppermute | solution.py:654
  27.2 16.8 %collective-permute-start.1 = (bf16[512,384]{1,0:T(8,128)(2,1)S(1)}, bf16[512,384]{1,0:T(8,128)(2,1)S(1)}, u32[]{:S(2)}, u32[]{:S(2)}) collective-permute-start(bf16[512,384]{1,0:T(8,128)(2,1)S(1)} %bitcast.18), channel_id=1, source_target_pairs={{0,32},{16,48},{32,0},{48,16},{64,96},{80,112},{96,64},{112,80},{1... | collective-permute-start | bytes 1179656 | tf_op jit(solution)/shard_map/ppermute | solution.py:654
  33.6 12.4 %all-to-all-start.1 = ((bf16[16,80,128]{2,1,0:T(8,128)(2,1)}), bf16[16,80,128]{2,1,0:T(8,128)(2,1)S(1)}, u32[]{:S(2)}, u32[]{:S(2)}) async-start(bf16[16,80,128]{2,1,0:T(8,128)(2,1)} %get-tuple-element.28), calls=%async_computation.1 | async-start | bytes 655360 | tf_op jit(solution)/shard_map/all_to_all | solution.py:658
  44.0 19.7 %copy-start.3 = (bf16[512,384]{1,0:T(8,128)(2,1)}, bf16[512,384]{1,0:T(8,128)(2,1)S(1)}, u32[]{:S(2)}) copy-start(bf16[512,384]{1,0:T(8,128)(2,1)S(1)} %collective-permute-done.3.refs_8_) | copy-start | bytes 1179652
  51.2 19.1 %all-to-all-start.2 = ((bf16[8,288,128]{2,1,0:T(8,128)(2,1)}), bf16[8,288,128]{2,1,0:T(8,128)(2,1)}, u32[]{:S(2)}, u32[]{:S(2)}) async-start(bf16[8,288,128]{2,1,0:T(8,128)(2,1)} %get-tuple-element.34), calls=%async_computation.2 | async-start | bytes 1179648 | tf_op jit(solution)/shard_map/all_to_all | solution.py:665
  60.0 4.3 %collective-permute-start.4 = (bf16[512,384]{1,0:T(8,128)(2,1)S(1)}, bf16[512,384]{1,0:T(8,128)(2,1)S(1)}, u32[]{:S(2)}, u32[]{:S(2)}) collective-permute-start(bf16[512,384]{1,0:T(8,128)(2,1)S(1)} %bitcast.19), channel_id=1, source_target_pairs={{0,16},{16,0},{32,48},{48,32},{64,80},{80,64},{96,112},{112,96},{1... | collective-permute-start | bytes 1179656 | tf_op jit(solution)/shard_map/ppermute | solution.py:654
  60.0 4.3 %collective-permute-start.5 = (bf16[512,384]{1,0:T(8,128)(2,1)S(1)}, bf16[512,384]{1,0:T(8,128)(2,1)S(1)}, u32[]{:S(2)}, u32[]{:S(2)}) collective-permute-start(bf16[512,384]{1,0:T(8,128)(2,1)S(1)} %collective-permute-done.1.refs_4_), channel_id=1, source_target_pairs={{0,16},{16,0},{32,48},{48,32},{64,80},{80,64},{96,112},{112,96},{1... | collective-permute-start | bytes 1179656 | tf_op jit(solution)/shard_map/ppermute | solution.py:654
  60.5 3.8 %collective-permute-start.6 = (bf16[512,384]{1,0:T(8,128)(2,1)S(1)}, bf16[512,384]{1,0:T(8,128)(2,1)}, u32[]{:S(2)}, u32[]{:S(2)}) collective-permute-start(bf16[512,384]{1,0:T(8,128)(2,1)S(1)} %collective-permute-done.2.refs_6_), channel_id=1, source_target_pairs={{0,16},{16,0},{32,48},{48,32},{64,80},{80,64},{96,112},{112,96},{1... | collective-permute-start | bytes 1179656 | tf_op jit(solution)/shard_map/ppermute | solution.py:654
  60.5 3.8 %collective-permute-start.7 = (bf16[512,384]{1,0:T(8,128)(2,1)S(1)}, bf16[512,384]{1,0:T(8,128)(2,1)}, u32[]{:S(2)}, u32[]{:S(2)}) collective-permute-start(bf16[512,384]{1,0:T(8,128)(2,1)S(1)} %collective-permute-done.3.refs_8_), channel_id=1, source_target_pairs={{0,16},{16,0},{32,48},{48,32},{64,80},{80,64},{96,112},{112,96},{1... | collective-permute-start | bytes 1179656 | tf_op jit(solution)/shard_map/ppermute | solution.py:654
  63.8 11.9 %collective-permute-start.8 = (bf16[16,512]{1,0:T(8,128)(2,1)S(1)}, bf16[16,512]{1,0:T(8,128)(2,1)S(1)}, u32[]{:S(2)}, u32[]{:S(2)}) collective-permute-start(bf16[16,512]{1,0:T(8,128)(2,1)S(1)} %get-tuple-element.42), channel_id=1, source_target_pairs={{0,1},{1,2},{2,3},{3,4},{4,5},{5,6},{6,7},{7,8},{8,9},{9,10},{10,1... | collective-permute-start | bytes 49160 | tf_op jit(solution)/shard_map/ppermute | solution.py:667
  75.7 23.3 %all-to-all-start.3 = ((bf16[128,32,128]{2,1,0:T(8,128)(2,1)}), bf16[128,32,128]{2,1,0:T(8,128)(2,1)S(1)}, u32[]{:S(2)}, u32[]{:S(2)}) async-start(bf16[128,32,128]{2,1,0:T(8,128)(2,1)} %terms.1), calls=%async_computation.3 | async-start | bytes 2097152 | tf_op jit(solution)/shard_map/all_to_all | solution.py:671
where the time goes:
time: 100 us; the launch traced here: 99.8 us
  starting transfers between devices  35.8 us (36%)
  waiting for transfers between devices  35 us (35%)
  Pallas kernels  24.9 us (25%)
  local copies, waits for them, and re-layouts  1.86 us (2%)
  between operations  1.42 us (1%)
    all_to_all x1, waiting for transfers between devices, per_device(): final = lax.all_to_all(terms, ('dp', 'seq'), 0, 0, tiled=True)  18.1 us
    all_to_all x1, starting transfers between devices, per_device(): grads = lax.all_to_all(message, 'dp', 0, 0, tiled=True)  8.81 us
    all_to_all x1, starting transfers between devices, per_device(): got = lax.all_to_all(message, 'seq', 0, 0, tiled=True)  6.37 us
    ppermute x7, waiting for transfers between devices, passed(): return lax.ppermute(value, 'dp', [(i, i ^ step) for i in range(8)])  6.02 us
    all_to_all x1, waiting for transfers between devices, per_device(): grads = lax.all_to_all(message, 'dp', 0, 0, tiled=True)  5.96 us
    ppermute x1, starting transfers between devices, edges(): lax.ppermute(first, 'seq', [(i, (i - 1) % count) for i in range(count)])  5.83 us
    pallas_call x1, Pallas kernels, forward_part(): pl.pallas_call(forward_kernel, out_shape=[jax.ShapeDtypeStruct((16, 80, 1...  5.77 us
    ppermute x7, starting transfers between devices, passed(): return lax.ppermute(value, 'dp', [(i, i ^ step) for i in range(8)])  5.52 us
  transfers between devices with their start and end apart: 13, of which 6 were waited for; matrix products, arithmetic and copies ran while one was open for 2% of the time, Pallas kernels for 12%

commit v1 on v0

--- a/solution.py
+++ b/solution.py
@@ -220,7 +220,7 @@
             pltpu.VMEM((288, 512), F32),
             pltpu.VMEM((160, 1024), F32),
             pltpu.VMEM((320, 512), F32),
-            pltpu.VMEM((1152, 128), F32),
+            pltpu.VMEM((1168, 128), F32),
             pltpu.VMEM((160, 512), F32),
             pltpu.SemaphoreType.DMA((7,)),
             pltpu.SemaphoreType.DMA((4,)),
@@ -440,7 +440,7 @@
             pltpu.VMEM((256, 512), F32),
             pltpu.VMEM((1, 16), F32),
             pltpu.VMEM((160, 1024), F32),
-            pltpu.VMEM((1152, 128), F32),
+            pltpu.VMEM((1168, 128), F32),
             pltpu.VMEM((288, 512), F32),
             pltpu.SemaphoreType.DMA((8,)),
             pltpu.SemaphoreType.DMA((5,)),
@@ -556,7 +556,7 @@
         )
         if owner < 4:
             mess[slot, 30:32, :] = head
-        out_ref[owner] = mess[slot].astype(BF)
+        out_ref[owner] = mess[slot, 0:32, :].astype(BF)
         if owner % 32 == 31:
             part = pl.ds(owner - 31, 32)
             sent.append(
@@ -582,9 +582,9 @@
             pltpu.VMEM((288, 128), F32),
             pltpu.VMEM((2048, 384), BF),
             pltpu.VMEM((1024, 640), BF),
-            pltpu.VMEM((2560, 128), F32),
-            pltpu.VMEM((2560, 128), F32),
-            pltpu.VMEM((4, 32, 128), F32),
+            pltpu.VMEM((2576, 128), F32),
+            pltpu.VMEM((2576, 128), F32),
+            pltpu.VMEM((4, 48, 128), F32),
             pltpu.SemaphoreType.DMA((10,)),
             pltpu.SemaphoreType.DMA((4,)),
         ],
@@ -606,8 +606,9 @@
             sums.append(total[20:30])
         one, two = sums
         lanes = slice(128 * pair, 128 * pair + 128)
-        first_ref[0:10, lanes] = jnp.where(left, one, swap(two))
-        first_ref[10:20, lanes] = jnp.where(left, swap(one), two)
+        first_ref[:, lanes] = jnp.concatenate(
+            [jnp.where(left, one, swap(two)), jnp.where(left, swap(one), two)], axis=0
+        )
     left = half_lanes(16)
     for pair in range(8):
         sums = []

time: 100 us -> 100 us (level)
  no operation moved by 1% of the time
where the time goes in v1:
time: 100 us; the launch traced here: 99.8 us
  starting transfers between devices  35.8 us (36%)
  waiting for transfers between devices  35.1 us (35%)
  Pallas kernels  24.8 us (25%)
  local copies, waits for them, and re-layouts  1.86 us (2%)
  between operations  1.42 us (1%)
    all_to_all x1, waiting for transfers between devices, per_device(): final = lax.all_to_all(terms, ('dp', 'seq'), 0, 0, tiled=True)  18.1 us
    all_to_all x1, starting transfers between devices, per_device(): grads = lax.all_to_all(message, 'dp', 0, 0, tiled=True)  8.81 us
    all_to_all x1, starting transfers between devices, per_device(): got = lax.all_to_all(message, 'seq', 0, 0, tiled=True)  6.38 us
    ppermute x7, waiting for transfers between devices, passed(): return lax.ppermute(value, 'dp', [(i, i ^ step) for i in range(8)])  6.02 us
    all_to_all x1, waiting for transfers between devices, per_device(): grads = lax.all_to_all(message, 'dp', 0, 0, tiled=True)  5.95 us
    ppermute x1, starting transfers between devices, edges(): lax.ppermute(first, 'seq', [(i, (i - 1) % count) for i in range(count)])  5.83 us
    pallas_call x1, Pallas kernels, forward_part(): pl.pallas_call(forward_kernel, out_shape=[jax.ShapeDtypeStruct((16, 80, 1...  5.78 us
    ppermute x7, starting transfers between devices, passed(): return lax.ppermute(value, 'dp', [(i, i ^ step) for i in range(8)])  5.51 us
  transfers between devices with their start and end apart: 13, of which 6 were waited for; matrix products, arithmetic and copies ran while one was open for 2% of the time, Pallas kernels for 12%

profile of v1, /device:TPU:1, one launch (start us, length us, event | category | flops | bytes accessed | tf_op | source)
XLA Modules:
  0.0 99.8 jit_solution(15664082770106837199)
XLA Ops:
  0.6 1.4 %edges.1 = bf16[48,512]{1,0:T(8,128)(2,1)} custom-call(bf16[256,512]{1,0:T(8,128)(2,1)} %bitcast.26, bf16[128,1024]{1,0:T(8,128)(2,1)} %bitcast.14), custom_call_target="tpu_custom_call" | custom-call | tf_op jit(solution)/shard_map/edges/pallas_call | solution.py:83
  2.1 5.8 %collective-permute-start = (bf16[48,512]{1,0:T(8,128)(2,1)}, bf16[48,512]{1,0:T(8,128)(2,1)S(1)}, u32[]{:S(2)}, u32[]{:S(2)}) collective-permute-start(bf16[48,512]{1,0:T(8,128)(2,1)} %edges.1), channel_id=1, source_target_pairs={{0,15},{1,0},{2,1},{3,2},{4,3},{5,4},{6,5},{7,6},{8,7},{9,8},{10,9... | collective-permute-start | bytes 147464 | tf_op jit(solution)/shard_map/ppermute | solution.py:97
  8.6 0.8 collective-permute-done.refs_1_
  9.4 0.6 copy-done.2
  10.0 5.8 %forward.1 = (bf16[16,80,128]{2,1,0:T(8,128)(2,1)}, bf16[384,512]{1,0:T(8,128)(2,1)}, f32[288,512]{1,0:T(8,128)}, f32[160,1024]{1,0:T(8,128)}) custom-call(s32[1]{0:T(128)} %bitcast.seq_ref, s32[1]{0:T(128)} %bitcast.12.live_ref, bf16[256,512]{1,0:T(8,128)(2,1)} %bitcast.27, bf16[48,512]{1,0:T(8,128)(2,1)} %copy-done.2, bf16[2560,512]{1,0:T(8,128)(2,1)} %bitcast.24, ...), custom_call_target="tpu_custom_call" | custom-call | flops 1500000000 | bytes 10000000 | tf_op jit(solution)/shard_map/forward/pallas_call | solution.py:200
  15.8 6.4 %all-to-all-start = ((bf16[16,80,128]{2,1,0:T(8,128)(2,1)}), bf16[16,80,128]{2,1,0:T(8,128)(2,1)S(1)}, u32[]{:S(2)}, u32[]{:S(2)}) async-start(bf16[16,80,128]{2,1,0:T(8,128)(2,1)} %get-tuple-element.27), calls=%async_computation | async-start | bytes 655360 | tf_op jit(solution)/shard_map/all_to_all | solution.py:650
  22.2 1.2 %copy.14 = bf16[384,512]{0,1:T(8,128)(2,1)S(1)} copy(bf16[384,512]{1,0:T(8,128)(2,1)} %get-tuple-element.29) | data formatting | bytes 786432 | tf_op jit(solution)/shard_map/forward/pallas_call | solution.py:200
  23.4 3.8 %collective-permute-start.3 = (bf16[512,384]{1,0:T(8,128)(2,1)S(1)}, bf16[512,384]{1,0:T(8,128)(2,1)S(1)}, u32[]{:S(2)}, u32[]{:S(2)}) collective-permute-start(bf16[512,384]{1,0:T(8,128)(2,1)S(1)} %bitcast.16), channel_id=1, source_target_pairs={{0,96},{16,112},{32,64},{48,80},{64,32},{80,48},{96,0},{112,16},{1... | collective-permute-start | bytes 1179656 | tf_op jit(solution)/shard_map/ppermute | solution.py:655
  27.2 0.0 collective-permute-start.2
  27.2 0.7 collective-permute-start.1
  27.9 2.2 %all-to-all-done.got_ref = bf16[16,80,128]{2,1,0:T(8,128)(2,1)S(1)} async-done(((bf16[16,80,128]{2,1,0:T(8,128)(2,1)}), bf16[16,80,128]{2,1,0:T(8,128)(2,1)S(1)}, u32[]{:S(2)}, u32[]{:S(2)}) %all-to-all-start) | async-done | bytes 327712 | tf_op jit(solution)/shard_map/all_to_all | solution.py:650
  30.1 3.4 %pairs.1 = (bf16[16,80,128]{2,1,0:T(8,128)(2,1)}, f32[1,128]{1,0:T(1,128)S(1)}) custom-call(s32[1]{0:T(128)} %bitcast.seq_ref, bf16[16,80,128]{2,1,0:T(8,128)(2,1)S(1)} %all-to-all-done.got_ref, f32[8,128]{1,0:T(8,128)S(1)} %bitcast.21), custom_call_target="tpu_custom_call" | custom-call | flops 500000000 | bytes 1000000 | tf_op jit(solution)/shard_map/pairs/pallas_call | solution.py:318
  33.6 4.4 %all-to-all-start.1 = ((bf16[16,80,128]{2,1,0:T(8,128)(2,1)}), bf16[16,80,128]{2,1,0:T(8,128)(2,1)S(1)}, u32[]{:S(2)}, u32[]{:S(2)}) async-start(bf16[16,80,128]{2,1,0:T(8,128)(2,1)} %get-tuple-element.28), calls=%async_computation.1 | async-start | bytes 655360 | tf_op jit(solution)/shard_map/all_to_all | solution.py:659
  38.0 6.0 %collective-permute-done.3.refs_8_ = bf16[512,384]{1,0:T(8,128)(2,1)S(1)} collective-permute-done((bf16[512,384]{1,0:T(8,128)(2,1)S(1)}, bf16[512,384]{1,0:T(8,128)(2,1)S(1)}, u32[]{:S(2)}, u32[]{:S(2)}) %collective-permute-start.3) | collective-permute-done | bytes 393248 | tf_op jit(solution)/shard_map/ppermute | solution.py:655
  44.1 1.9 %all-to-all-done.1.back_ref = bf16[16,80,128]{2,1,0:T(8,128)(2,1)S(1)} async-done(((bf16[16,80,128]{2,1,0:T(8,128)(2,1)}), bf16[16,80,128]{2,1,0:T(8,128)(2,1)S(1)}, u32[]{:S(2)}, u32[]{:S(2)}) %all-to-all-start.1) | async-done | bytes 327712 | tf_op jit(solution)/shard_map/all_to_all | solution.py:659
  45.9 5.2 %backward.1 = (bf16[8,288,128]{2,1,0:T(8,128)(2,1)}, bf16[288,512]{1,0:T(8,128)(2,1)S(1)}, f32[256,512]{1,0:T(8,128)S(1)}, f32[1,16]{1,0:T(1,128)}) custom-call(s32[1]{0:T(128)} %bitcast.seq_ref, s32[1]{0:T(128)} %bitcast.13.live_ref, bf16[16,80,128]{2,1,0:T(8,128)(2,1)S(1)} %all-to-all-done.1.back_ref, bf16[128,1024]{1,0:T(8,128)(2,1)S(1)} %bitcast.15, ...), custom_call_target="tpu_custom_call" | custom-call | flops 800000000 | bytes 10000000 | tf_op jit(solution)/shard_map/backward/pallas_call | solution.py:423
  51.2 8.8 %all-to-all-start.2 = ((bf16[8,288,128]{2,1,0:T(8,128)(2,1)}), bf16[8,288,128]{2,1,0:T(8,128)(2,1)}, u32[]{:S(2)}, u32[]{:S(2)}) async-start(bf16[8,288,128]{2,1,0:T(8,128)(2,1)} %get-tuple-element.34), calls=%async_computation.2 | async-start | bytes 1179648 | tf_op jit(solution)/shard_map/all_to_all | solution.py:666
  60.0 0.0 collective-permute-start.4
  60.0 0.5 collective-permute-start.5
  60.5 0.0 collective-permute-start.6
  60.5 0.5 collective-permute-start.7
  61.0 2.7 %inputs.1 = (bf16[256,512]{1,0:T(8,128)(2,1)S(1)}, bf16[16,512]{1,0:T(8,128)(2,1)S(1)}) custom-call(s32[1]{0:T(128)} %bitcast.seq_ref, bf16[288,512]{1,0:T(8,128)(2,1)S(1)} %get-tuple-element.40.refs_0_, f32[256,512]{1,0:T(8,128)S(1)} %get-tuple-element.41.refs_1_, bf16[2560,512]{1,0:T(8,128)(2,1)} %bitcast.25), custom_call_target="tpu_custom_call" | custom-call | flops 700000000 | bytes 4000000 | tf_op jit(solution)/shard_map/inputs/pallas_call | solution.py:477
  63.8 0.5 collective-permute-start.8
  64.3 0.0 collective-permute-done.4.refs_3_
  64.3 0.0 collective-permute-done.7.refs_9_
  64.3 6.0 %all-to-all-done.2.refs_0_ = bf16[8,288,128]{2,1,0:T(8,128)(2,1)} async-done(((bf16[8,288,128]{2,1,0:T(8,128)(2,1)}), bf16[8,288,128]{2,1,0:T(8,128)(2,1)}, u32[]{:S(2)}, u32[]{:S(2)}) %all-to-all-start.2) | async-done | bytes 589856 | tf_op jit(solution)/shard_map/all_to_all | solution.py:666
  70.3 5.4 %terms.1 = bf16[128,32,128]{2,1,0:T(8,128)(2,1)} custom-call(s32[1]{0:T(128)} %bitcast.8.dp_ref, s32[1]{0:T(128)} %bitcast.seq_ref, bf16[8,288,128]{2,1,0:T(8,128)(2,1)} %all-to-all-done.2.refs_0_, f32[1,128]{1,0:T(1,128)S(1)} %get-tuple-element.35.refs_1_, bf16[512,384]{1,0:T(8,128)(2,1)S(1)} %bitcast.20, ...), custom_call_target="tpu_custom_call" | custom-call | flops 3000000000 | bytes 5000000 | tf_op jit(solution)/shard_map/terms/pallas_call | solution.py:570
  75.7 0.0 collective-permute-done.8
  75.7 4.3 %all-to-all-start.3 = ((bf16[128,32,128]{2,1,0:T(8,128)(2,1)}), bf16[128,32,128]{2,1,0:T(8,128)(2,1)S(1)}, u32[]{:S(2)}, u32[]{:S(2)}) async-start(bf16[128,32,128]{2,1,0:T(8,128)(2,1)} %terms.1), calls=%async_computation.3 | async-start | bytes 2097152 | tf_op jit(solution)/shard_map/all_to_all | solution.py:672
  80.0 0.8 maximum_bitcast_fusion
  80.8 18.1 %all-to-all-done.3.final_ref = bf16[128,32,128]{2,1,0:T(8,128)(2,1)S(1)} async-done(((bf16[128,32,128]{2,1,0:T(8,128)(2,1)}), bf16[128,32,128]{2,1,0:T(8,128)(2,1)S(1)}, u32[]{:S(2)}, u32[]{:S(2)}) %all-to-all-start.3) | async-done | bytes 1048608 | tf_op jit(solution)/shard_map/all_to_all | solution.py:672
  98.9 0.8 final.1
  (13 shorter events, 0.0 us)
Async XLA Ops:
  0.6 29.5 %copy-start.1 = (f32[1024]{0:T(1024)S(1)}, f32[1024]{0:T(1024)}, u32[]{:S(2)}) copy-start(f32[1024]{0:T(1024)} %param.12) | copy-start | bytes 12292
  2.1 7.3 %collective-permute-start = (bf16[48,512]{1,0:T(8,128)(2,1)}, bf16[48,512]{1,0:T(8,128)(2,1)S(1)}, u32[]{:S(2)}, u32[]{:S(2)}) collective-permute-start(bf16[48,512]{1,0:T(8,128)(2,1)} %edges.1), channel_id=1, source_target_pairs={{0,15},{1,0},{2,1},{3,2},{4,3},{5,4},{6,5},{7,6},{8,7},{9,8},{10,9... | collective-permute-start | bytes 147464 | tf_op jit(solution)/shard_map/ppermute | solution.py:97
  9.4 0.6 copy-start.2
  10.0 35.9 %copy-start = (bf16[1,128,1024]{2,1,0:T(8,128)(2,1)S(1)}, bf16[1,128,1024]{2,1,0:T(8,128)(2,1)}, u32[]{:S(2)}) copy-start(bf16[1,128,1024]{2,1,0:T(8,128)(2,1)} %param.13) | copy-start | bytes 786436
  15.8 14.3 %all-to-all-start = ((bf16[16,80,128]{2,1,0:T(8,128)(2,1)}), bf16[16,80,128]{2,1,0:T(8,128)(2,1)S(1)}, u32[]{:S(2)}, u32[]{:S(2)}) async-start(bf16[16,80,128]{2,1,0:T(8,128)(2,1)} %get-tuple-element.27), calls=%async_computation | async-start | bytes 655360 | tf_op jit(solution)/shard_map/all_to_all | solution.py:650
  23.4 20.6 %collective-permute-start.3 = (bf16[512,384]{1,0:T(8,128)(2,1)S(1)}, bf16[512,384]{1,0:T(8,128)(2,1)S(1)}, u32[]{:S(2)}, u32[]{:S(2)}) collective-permute-start(bf16[512,384]{1,0:T(8,128)(2,1)S(1)} %bitcast.16), channel_id=1, source_target_pairs={{0,96},{16,112},{32,64},{48,80},{64,32},{80,48},{96,0},{112,16},{1... | collective-permute-start | bytes 1179656 | tf_op jit(solution)/shard_map/ppermute | solution.py:655
  27.2 16.8 %collective-permute-start.2 = (bf16[512,384]{1,0:T(8,128)(2,1)S(1)}, bf16[512,384]{1,0:T(8,128)(2,1)S(1)}, u32[]{:S(2)}, u32[]{:S(2)}) collective-permute-start(bf16[512,384]{1,0:T(8,128)(2,1)S(1)} %bitcast.17), channel_id=1, source_target_pairs={{0,64},{16,80},{32,96},{48,112},{64,0},{80,16},{96,32},{112,48},{1... | collective-permute-start | bytes 1179656 | tf_op jit(solution)/shard_map/ppermute | solution.py:655
  27.2 16.8 %collective-permute-start.1 = (bf16[512,384]{1,0:T(8,128)(2,1)S(1)}, bf16[512,384]{1,0:T(8,128)(2,1)S(1)}, u32[]{:S(2)}, u32[]{:S(2)}) collective-permute-start(bf16[512,384]{1,0:T(8,128)(2,1)S(1)} %bitcast.18), channel_id=1, source_target_pairs={{0,32},{16,48},{32,0},{48,16},{64,96},{80,112},{96,64},{112,80},{1... | collective-permute-start | bytes 1179656 | tf_op jit(solution)/shard_map/ppermute | solution.py:655
  33.6 12.3 %all-to-all-start.1 = ((bf16[16,80,128]{2,1,0:T(8,128)(2,1)}), bf16[16,80,128]{2,1,0:T(8,128)(2,1)S(1)}, u32[]{:S(2)}, u32[]{:S(2)}) async-start(bf16[16,80,128]{2,1,0:T(8,128)(2,1)} %get-tuple-element.28), calls=%async_computation.1 | async-start | bytes 655360 | tf_op jit(solution)/shard_map/all_to_all | solution.py:659
  44.0 19.7 %copy-start.3 = (bf16[512,384]{1,0:T(8,128)(2,1)}, bf16[512,384]{1,0:T(8,128)(2,1)S(1)}, u32[]{:S(2)}) copy-start(bf16[512,384]{1,0:T(8,128)(2,1)S(1)} %collective-permute-done.3.refs_8_) | copy-start | bytes 1179652
  51.2 19.1 %all-to-all-start.2 = ((bf16[8,288,128]{2,1,0:T(8,128)(2,1)}), bf16[8,288,128]{2,1,0:T(8,128)(2,1)}, u32[]{:S(2)}, u32[]{:S(2)}) async-start(bf16[8,288,128]{2,1,0:T(8,128)(2,1)} %get-tuple-element.34), calls=%async_computation.2 | async-start | bytes 1179648 | tf_op jit(solution)/shard_map/all_to_all | solution.py:666
  60.0 4.3 %collective-permute-start.4 = (bf16[512,384]{1,0:T(8,128)(2,1)S(1)}, bf16[512,384]{1,0:T(8,128)(2,1)S(1)}, u32[]{:S(2)}, u32[]{:S(2)}) collective-permute-start(bf16[512,384]{1,0:T(8,128)(2,1)S(1)} %bitcast.19), channel_id=1, source_target_pairs={{0,16},{16,0},{32,48},{48,32},{64,80},{80,64},{96,112},{112,96},{1... | collective-permute-start | bytes 1179656 | tf_op jit(solution)/shard_map/ppermute | solution.py:655
  60.0 4.3 %collective-permute-start.5 = (bf16[512,384]{1,0:T(8,128)(2,1)S(1)}, bf16[512,384]{1,0:T(8,128)(2,1)S(1)}, u32[]{:S(2)}, u32[]{:S(2)}) collective-permute-start(bf16[512,384]{1,0:T(8,128)(2,1)S(1)} %collective-permute-done.1.refs_4_), channel_id=1, source_target_pairs={{0,16},{16,0},{32,48},{48,32},{64,80},{80,64},{96,112},{112,96},{1... | collective-permute-start | bytes 1179656 | tf_op jit(solution)/shard_map/ppermute | solution.py:655
  60.5 3.8 %collective-permute-start.6 = (bf16[512,384]{1,0:T(8,128)(2,1)S(1)}, bf16[512,384]{1,0:T(8,128)(2,1)}, u32[]{:S(2)}, u32[]{:S(2)}) collective-permute-start(bf16[512,384]{1,0:T(8,128)(2,1)S(1)} %collective-permute-done.2.refs_6_), channel_id=1, source_target_pairs={{0,16},{16,0},{32,48},{48,32},{64,80},{80,64},{96,112},{112,96},{1... | collective-permute-start | bytes 1179656 | tf_op jit(solution)/shard_map/ppermute | solution.py:655
  60.5 3.8 %collective-permute-start.7 = (bf16[512,384]{1,0:T(8,128)(2,1)S(1)}, bf16[512,384]{1,0:T(8,128)(2,1)}, u32[]{:S(2)}, u32[]{:S(2)}) collective-permute-start(bf16[512,384]{1,0:T(8,128)(2,1)S(1)} %collective-permute-done.3.refs_8_), channel_id=1, source_target_pairs={{0,16},{16,0},{32,48},{48,32},{64,80},{80,64},{96,112},{112,96},{1... | collective-permute-start | bytes 1179656 | tf_op jit(solution)/shard_map/ppermute | solution.py:655
  63.8 11.9 %collective-permute-start.8 = (bf16[16,512]{1,0:T(8,128)(2,1)S(1)}, bf16[16,512]{1,0:T(8,128)(2,1)S(1)}, u32[]{:S(2)}, u32[]{:S(2)}) collective-permute-start(bf16[16,512]{1,0:T(8,128)(2,1)S(1)} %get-tuple-element.42), channel_id=1, source_target_pairs={{0,1},{1,2},{2,3},{3,4},{4,5},{5,6},{6,7},{7,8},{8,9},{9,10},{10,1... | collective-permute-start | bytes 49160 | tf_op jit(solution)/shard_map/ppermute | solution.py:668
  75.7 23.3 %all-to-all-start.3 = ((bf16[128,32,128]{2,1,0:T(8,128)(2,1)}), bf16[128,32,128]{2,1,0:T(8,128)(2,1)S(1)}, u32[]{:S(2)}, u32[]{:S(2)}) async-start(bf16[128,32,128]{2,1,0:T(8,128)(2,1)} %terms.1), calls=%async_computation.3 | async-start | bytes 2097152 | tf_op jit(solution)/shard_map/all_to_all | solution.py:672

commit v2 on v1

--- a/solution.py
+++ b/solution.py
@@ -184,15 +184,22 @@
     ):
         info = jnp.where(lane == place, value, info)
     info = info.astype(BF)
+    for target in range(16):
+        mess_ref[target, 64:80, :] = info
     left = half_lanes(64)
     for pair in range(8):
         top = act[8:72, 128 * pair : 128 * pair + 128]
         low = act[72:136, 128 * pair : 128 * pair + 128]
         mess_ref[2 * pair, 0:64, :] = jnp.where(left, top, swap(low)).astype(BF)
         mess_ref[2 * pair + 1, 0:64, :] = jnp.where(left, swap(top), low).astype(BF)
-    for target in range(16):
-        mess_ref[target, 64:80, :] = info
-    sent.append(send(0))
+        if pair % 2 == 1:
+            part = pl.ds(2 * pair - 2, 4)
+            sent.append(
+                pltpu.make_async_copy(
+                    mess_ref.at[part], outs[0].at[part], out_sems.at[4 + pair // 2]
+                )
+            )
+            sent[-1].start()
     wait_for(sent)
 
 
@@ -223,7 +230,7 @@
             pltpu.VMEM((1168, 128), F32),
             pltpu.VMEM((160, 512), F32),
             pltpu.SemaphoreType.DMA((7,)),
-            pltpu.SemaphoreType.DMA((4,)),
+            pltpu.SemaphoreType.DMA((8,)),
         ],
         compiler_params=pltpu.CompilerParams(vmem_limit_bytes=56 * MEBI),
         cost_estimate=pl.CostEstimate(
@@ -407,7 +414,8 @@
         two = grad_1[136:280, lanes]
         mess_ref[2 * pair, 0:144, :] = jnp.where(left, one, swap(two)).astype(BF)
         mess_ref[2 * pair + 1, 0:144, :] = jnp.where(left, swap(one), two).astype(BF)
-    sent.append(send(0, lambda ref: ref.at[:, pl.ds(0, 144)], 3))
+        part = pl.ds(2 * pair, 2)
+        sent.append(send(0, lambda ref, part=part: ref.at[part, pl.ds(0, 144)], 5 + pair))
     total = jnp.zeros((16, 128), F32)
     for source in range(16):
         total = total + back_ref[source, 64:80, :].astype(F32)
@@ -443,7 +451,7 @@
             pltpu.VMEM((1168, 128), F32),
             pltpu.VMEM((288, 512), F32),
             pltpu.SemaphoreType.DMA((8,)),
-            pltpu.SemaphoreType.DMA((5,)),
+            pltpu.SemaphoreType.DMA((9,)),
         ],
         compiler_params=pltpu.CompilerParams(vmem_limit_bytes=52 * MEBI),
         cost_estimate=pl.CostEstimate(

time: 100 us -> 100 us (level)
  no operation moved by 1% of the time
where the time goes in v2:
time: 100 us; the launch traced here: 99.8 us
  starting transfers between devices  35.8 us (36%)
  waiting for transfers between devices  35 us (35%)
  Pallas kernels  24.9 us (25%)
  local copies, waits for them, and re-layouts  1.86 us (2%)
  between operations  1.42 us (1%)
    all_to_all x1, waiting for transfers between devices, per_device(): final = lax.all_to_all(terms, ('dp', 'seq'), 0, 0, tiled=True)  18.1 us
    all_to_all x1, starting transfers between devices, per_device(): grads = lax.all_to_all(message, 'dp', 0, 0, tiled=True)  8.81 us
    all_to_all x1, starting transfers between devices, per_device(): got = lax.all_to_all(message, 'seq', 0, 0, tiled=True)  6.38 us
    ppermute x7, waiting for transfers between devices, passed(): return lax.ppermute(value, 'dp', [(i, i ^ step) for i in range(8)])  6.02 us
    all_to_all x1, waiting for transfers between devices, per_device(): grads = lax.all_to_all(message, 'dp', 0, 0, tiled=True)  5.95 us
    ppermute x1, starting transfers between devices, edges(): lax.ppermute(first, 'seq', [(i, (i - 1) % count) for i in range(count)])  5.83 us
    pallas_call x1, Pallas kernels, forward_part(): pl.pallas_call(forward_kernel, out_shape=[jax.ShapeDtypeStruct((16, 80, 1...  5.82 us
    ppermute x7, starting transfers between devices, passed(): return lax.ppermute(value, 'dp', [(i, i ^ step) for i in range(8)])  5.51 us
  transfers between devices with their start and end apart: 13, of which 6 were waited for; matrix products, arithmetic and copies ran while one was open for 2% of the time, Pallas kernels for 12%

profile of v2, /device:TPU:1, one launch (start us, length us, event | category | flops | bytes accessed | tf_op | source)
XLA Modules:
  0.0 99.8 jit_solution(14568983202154341356)
XLA Ops:
  0.6 1.4 %edges.1 = bf16[48,512]{1,0:T(8,128)(2,1)} custom-call(bf16[256,512]{1,0:T(8,128)(2,1)} %bitcast.26, bf16[128,1024]{1,0:T(8,128)(2,1)} %bitcast.14), custom_call_target="tpu_custom_call" | custom-call | tf_op jit(solution)/shard_map/edges/pallas_call | solution.py:83
  2.1 5.8 %collective-permute-start = (bf16[48,512]{1,0:T(8,128)(2,1)}, bf16[48,512]{1,0:T(8,128)(2,1)S(1)}, u32[]{:S(2)}, u32[]{:S(2)}) collective-permute-start(bf16[48,512]{1,0:T(8,128)(2,1)} %edges.1), channel_id=1, source_target_pairs={{0,15},{1,0},{2,1},{3,2},{4,3},{5,4},{6,5},{7,6},{8,7},{9,8},{10,9... | collective-permute-start | bytes 147464 | tf_op jit(solution)/shard_map/ppermute | solution.py:97
  8.6 0.8 collective-permute-done.refs_1_
  9.4 0.6 copy-done.2
  10.0 5.8 %forward.1 = (bf16[16,80,128]{2,1,0:T(8,128)(2,1)}, bf16[384,512]{1,0:T(8,128)(2,1)}, f32[288,512]{1,0:T(8,128)}, f32[160,1024]{1,0:T(8,128)}) custom-call(s32[1]{0:T(128)} %bitcast.seq_ref, s32[1]{0:T(128)} %bitcast.12.live_ref, bf16[256,512]{1,0:T(8,128)(2,1)} %bitcast.27, bf16[48,512]{1,0:T(8,128)(2,1)} %copy-done.2, bf16[2560,512]{1,0:T(8,128)(2,1)} %bitcast.24, ...), custom_call_target="tpu_custom_call" | custom-call | flops 1500000000 | bytes 10000000 | tf_op jit(solution)/shard_map/forward/pallas_call | solution.py:207
  15.9 6.4 %all-to-all-start = ((bf16[16,80,128]{2,1,0:T(8,128)(2,1)}), bf16[16,80,128]{2,1,0:T(8,128)(2,1)S(1)}, u32[]{:S(2)}, u32[]{:S(2)}) async-start(bf16[16,80,128]{2,1,0:T(8,128)(2,1)} %get-tuple-element.27), calls=%async_computation | async-start | bytes 655360 | tf_op jit(solution)/shard_map/all_to_all | solution.py:658
  22.2 1.2 %copy.14 = bf16[384,512]{0,1:T(8,128)(2,1)S(1)} copy(bf16[384,512]{1,0:T(8,128)(2,1)} %get-tuple-element.29) | data formatting | bytes 786432 | tf_op jit(solution)/shard_map/forward/pallas_call | solution.py:207
  23.5 3.8 %collective-permute-start.3 = (bf16[512,384]{1,0:T(8,128)(2,1)S(1)}, bf16[512,384]{1,0:T(8,128)(2,1)S(1)}, u32[]{:S(2)}, u32[]{:S(2)}) collective-permute-start(bf16[512,384]{1,0:T(8,128)(2,1)S(1)} %bitcast.16), channel_id=1, source_target_pairs={{0,96},{16,112},{32,64},{48,80},{64,32},{80,48},{96,0},{112,16},{1... | collective-permute-start | bytes 1179656 | tf_op jit(solution)/shard_map/ppermute | solution.py:663
  27.3 0.0 collective-permute-start.2
  27.3 0.7 collective-permute-start.1
  27.9 2.2 %all-to-all-done.got_ref = bf16[16,80,128]{2,1,0:T(8,128)(2,1)S(1)} async-done(((bf16[16,80,128]{2,1,0:T(8,128)(2,1)}), bf16[16,80,128]{2,1,0:T(8,128)(2,1)S(1)}, u32[]{:S(2)}, u32[]{:S(2)}) %all-to-all-start) | async-done | bytes 327712 | tf_op jit(solution)/shard_map/all_to_all | solution.py:658
  30.2 3.4 %pairs.1 = (bf16[16,80,128]{2,1,0:T(8,128)(2,1)}, f32[1,128]{1,0:T(1,128)S(1)}) custom-call(s32[1]{0:T(128)} %bitcast.seq_ref, bf16[16,80,128]{2,1,0:T(8,128)(2,1)S(1)} %all-to-all-done.got_ref, f32[8,128]{1,0:T(8,128)S(1)} %bitcast.21), custom_call_target="tpu_custom_call" | custom-call | flops 500000000 | bytes 1000000 | tf_op jit(solution)/shard_map/pairs/pallas_call | solution.py:325
  33.6 4.4 %all-to-all-start.1 = ((bf16[16,80,128]{2,1,0:T(8,128)(2,1)}), bf16[16,80,128]{2,1,0:T(8,128)(2,1)S(1)}, u32[]{:S(2)}, u32[]{:S(2)}) async-start(bf16[16,80,128]{2,1,0:T(8,128)(2,1)} %get-tuple-element.28), calls=%async_computation.1 | async-start | bytes 655360 | tf_op jit(solution)/shard_map/all_to_all | solution.py:667
  38.1 6.0 %collective-permute-done.3.refs_8_ = bf16[512,384]{1,0:T(8,128)(2,1)S(1)} collective-permute-done((bf16[512,384]{1,0:T(8,128)(2,1)S(1)}, bf16[512,384]{1,0:T(8,128)(2,1)S(1)}, u32[]{:S(2)}, u32[]{:S(2)}) %collective-permute-start.3) | collective-permute-done | bytes 393248 | tf_op jit(solution)/shard_map/ppermute | solution.py:663
  44.1 0.0 collective-permute-done.2.refs_6_
  44.1 0.0 collective-permute-done.1.refs_4_
  44.1 1.9 %all-to-all-done.1.back_ref = bf16[16,80,128]{2,1,0:T(8,128)(2,1)S(1)} async-done(((bf16[16,80,128]{2,1,0:T(8,128)(2,1)}), bf16[16,80,128]{2,1,0:T(8,128)(2,1)S(1)}, u32[]{:S(2)}, u32[]{:S(2)}) %all-to-all-start.1) | async-done | bytes 327712 | tf_op jit(solution)/shard_map/all_to_all | solution.py:667
  46.0 5.2 %backward.1 = (bf16[8,288,128]{2,1,0:T(8,128)(2,1)}, bf16[288,512]{1,0:T(8,128)(2,1)S(1)}, f32[256,512]{1,0:T(8,128)S(1)}, f32[1,16]{1,0:T(1,128)}) custom-call(s32[1]{0:T(128)} %bitcast.seq_ref, s32[1]{0:T(128)} %bitcast.13.live_ref, bf16[16,80,128]{2,1,0:T(8,128)(2,1)S(1)} %all-to-all-done.1.back_ref, bf16[128,1024]{1,0:T(8,128)(2,1)S(1)} %bitcast.15, ...), custom_call_target="tpu_custom_call" | custom-call | flops 800000000 | bytes 10000000 | tf_op jit(solution)/shard_map/backward/pallas_call | solution.py:431
  51.2 8.8 %all-to-all-start.2 = ((bf16[8,288,128]{2,1,0:T(8,128)(2,1)}), bf16[8,288,128]{2,1,0:T(8,128)(2,1)}, u32[]{:S(2)}, u32[]{:S(2)}) async-start(bf16[8,288,128]{2,1,0:T(8,128)(2,1)} %get-tuple-element.34), calls=%async_computation.2 | async-start | bytes 1179648 | tf_op jit(solution)/shard_map/all_to_all | solution.py:674
  60.0 0.0 collective-permute-start.4
  60.0 0.5 collective-permute-start.5
  60.5 0.0 collective-permute-start.6
  60.5 0.5 collective-permute-start.7
  61.0 2.7 %inputs.1 = (bf16[256,512]{1,0:T(8,128)(2,1)S(1)}, bf16[16,512]{1,0:T(8,128)(2,1)S(1)}) custom-call(s32[1]{0:T(128)} %bitcast.seq_ref, bf16[288,512]{1,0:T(8,128)(2,1)S(1)} %get-tuple-element.40.refs_0_, f32[256,512]{1,0:T(8,128)S(1)} %get-tuple-element.41.refs_1_, bf16[2560,512]{1,0:T(8,128)(2,1)} %bitcast.25), custom_call_target="tpu_custom_call" | custom-call | flops 700000000 | bytes 4000000 | tf_op jit(solution)/shard_map/inputs/pallas_call | solution.py:485
  63.8 0.5 collective-permute-start.8
  64.3 0.0 collective-permute-done.4.refs_3_
  64.4 5.9 %all-to-all-done.2.refs_0_ = bf16[8,288,128]{2,1,0:T(8,128)(2,1)} async-done(((bf16[8,288,128]{2,1,0:T(8,128)(2,1)}), bf16[8,288,128]{2,1,0:T(8,128)(2,1)}, u32[]{:S(2)}, u32[]{:S(2)}) %all-to-all-start.2) | async-done | bytes 589856 | tf_op jit(solution)/shard_map/all_to_all | solution.py:674
  70.3 5.4 %terms.1 = bf16[128,32,128]{2,1,0:T(8,128)(2,1)} custom-call(s32[1]{0:T(128)} %bitcast.8.dp_ref, s32[1]{0:T(128)} %bitcast.seq_ref, bf16[8,288,128]{2,1,0:T(8,128)(2,1)} %all-to-all-done.2.refs_0_, f32[1,128]{1,0:T(1,128)S(1)} %get-tuple-element.35.refs_1_, bf16[512,384]{1,0:T(8,128)(2,1)S(1)} %bitcast.20, ...), custom_call_target="tpu_custom_call" | custom-call | flops 3000000000 | bytes 5000000 | tf_op jit(solution)/shard_map/terms/pallas_call | solution.py:578
  75.7 4.3 %all-to-all-start.3 = ((bf16[128,32,128]{2,1,0:T(8,128)(2,1)}), bf16[128,32,128]{2,1,0:T(8,128)(2,1)S(1)}, u32[]{:S(2)}, u32[]{:S(2)}) async-start(bf16[128,32,128]{2,1,0:T(8,128)(2,1)} %terms.1), calls=%async_computation.3 | async-start | bytes 2097152 | tf_op jit(solution)/shard_map/all_to_all | solution.py:680
  80.1 0.8 maximum_bitcast_fusion
  80.8 18.1 %all-to-all-done.3.final_ref = bf16[128,32,128]{2,1,0:T(8,128)(2,1)S(1)} async-done(((bf16[128,32,128]{2,1,0:T(8,128)(2,1)}), bf16[128,32,128]{2,1,0:T(8,128)(2,1)S(1)}, u32[]{:S(2)}, u32[]{:S(2)}) %all-to-all-start.3) | async-done | bytes 1048608 | tf_op jit(solution)/shard_map/all_to_all | solution.py:680
  98.9 0.8 final.1
  (13 shorter events, 0.1 us)
Async XLA Ops:
  0.6 29.5 %copy-start.1 = (f32[1024]{0:T(1024)S(1)}, f32[1024]{0:T(1024)}, u32[]{:S(2)}) copy-start(f32[1024]{0:T(1024)} %param.12) | copy-start | bytes 12292
  2.1 7.3 %collective-permute-start = (bf16[48,512]{1,0:T(8,128)(2,1)}, bf16[48,512]{1,0:T(8,128)(2,1)S(1)}, u32[]{:S(2)}, u32[]{:S(2)}) collective-permute-start(bf16[48,512]{1,0:T(8,128)(2,1)} %edges.1), channel_id=1, source_target_pairs={{0,15},{1,0},{2,1},{3,2},{4,3},{5,4},{6,5},{7,6},{8,7},{9,8},{10,9... | collective-permute-start | bytes 147464 | tf_op jit(solution)/shard_map/ppermute | solution.py:97
  9.4 0.6 copy-start.2
  10.0 35.9 %copy-start = (bf16[1,128,1024]{2,1,0:T(8,128)(2,1)S(1)}, bf16[1,128,1024]{2,1,0:T(8,128)(2,1)}, u32[]{:S(2)}) copy-start(bf16[1,128,1024]{2,1,0:T(8,128)(2,1)} %param.13) | copy-start | bytes 786436
  15.9 14.3 %all-to-all-start = ((bf16[16,80,128]{2,1,0:T(8,128)(2,1)}), bf16[16,80,128]{2,1,0:T(8,128)(2,1)S(1)}, u32[]{:S(2)}, u32[]{:S(2)}) async-start(bf16[16,80,128]{2,1,0:T(8,128)(2,1)} %get-tuple-element.27), calls=%async_computation | async-start | bytes 655360 | tf_op jit(solution)/shard_map/all_to_all | solution.py:658
  23.5 20.6 %collective-permute-start.3 = (bf16[512,384]{1,0:T(8,128)(2,1)S(1)}, bf16[512,384]{1,0:T(8,128)(2,1)S(1)}, u32[]{:S(2)}, u32[]{:S(2)}) collective-permute-start(bf16[512,384]{1,0:T(8,128)(2,1)S(1)} %bitcast.16), channel_id=1, source_target_pairs={{0,96},{16,112},{32,64},{48,80},{64,32},{80,48},{96,0},{112,16},{1... | collective-permute-start | bytes 1179656 | tf_op jit(solution)/shard_map/ppermute | solution.py:663
  27.3 16.8 %collective-permute-start.2 = (bf16[512,384]{1,0:T(8,128)(2,1)S(1)}, bf16[512,384]{1,0:T(8,128)(2,1)S(1)}, u32[]{:S(2)}, u32[]{:S(2)}) collective-permute-start(bf16[512,384]{1,0:T(8,128)(2,1)S(1)} %bitcast.17), channel_id=1, source_target_pairs={{0,64},{16,80},{32,96},{48,112},{64,0},{80,16},{96,32},{112,48},{1... | collective-permute-start | bytes 1179656 | tf_op jit(solution)/shard_map/ppermute | solution.py:663
  27.3 16.8 %collective-permute-start.1 = (bf16[512,384]{1,0:T(8,128)(2,1)S(1)}, bf16[512,384]{1,0:T(8,128)(2,1)S(1)}, u32[]{:S(2)}, u32[]{:S(2)}) collective-permute-start(bf16[512,384]{1,0:T(8,128)(2,1)S(1)} %bitcast.18), channel_id=1, source_target_pairs={{0,32},{16,48},{32,0},{48,16},{64,96},{80,112},{96,64},{112,80},{1... | collective-permute-start | bytes 1179656 | tf_op jit(solution)/shard_map/ppermute | solution.py:663
  33.6 12.3 %all-to-all-start.1 = ((bf16[16,80,128]{2,1,0:T(8,128)(2,1)}), bf16[16,80,128]{2,1,0:T(8,128)(2,1)S(1)}, u32[]{:S(2)}, u32[]{:S(2)}) async-start(bf16[16,80,128]{2,1,0:T(8,128)(2,1)} %get-tuple-element.28), calls=%async_computation.1 | async-start | bytes 655360 | tf_op jit(solution)/shard_map/all_to_all | solution.py:667
  44.1 19.7 %copy-start.3 = (bf16[512,384]{1,0:T(8,128)(2,1)}, bf16[512,384]{1,0:T(8,128)(2,1)S(1)}, u32[]{:S(2)}) copy-start(bf16[512,384]{1,0:T(8,128)(2,1)S(1)} %collective-permute-done.3.refs_8_) | copy-start | bytes 1179652
  51.2 19.1 %all-to-all-start.2 = ((bf16[8,288,128]{2,1,0:T(8,128)(2,1)}), bf16[8,288,128]{2,1,0:T(8,128)(2,1)}, u32[]{:S(2)}, u32[]{:S(2)}) async-start(bf16[8,288,128]{2,1,0:T(8,128)(2,1)} %get-tuple-element.34), calls=%async_computation.2 | async-start | bytes 1179648 | tf_op jit(solution)/shard_map/all_to_all | solution.py:674
  60.0 4.3 %collective-permute-start.4 = (bf16[512,384]{1,0:T(8,128)(2,1)S(1)}, bf16[512,384]{1,0:T(8,128)(2,1)S(1)}, u32[]{:S(2)}, u32[]{:S(2)}) collective-permute-start(bf16[512,384]{1,0:T(8,128)(2,1)S(1)} %bitcast.19), channel_id=1, source_target_pairs={{0,16},{16,0},{32,48},{48,32},{64,80},{80,64},{96,112},{112,96},{1... | collective-permute-start | bytes 1179656 | tf_op jit(solution)/shard_map/ppermute | solution.py:663
  60.0 4.3 %collective-permute-start.5 = (bf16[512,384]{1,0:T(8,128)(2,1)S(1)}, bf16[512,384]{1,0:T(8,128)(2,1)S(1)}, u32[]{:S(2)}, u32[]{:S(2)}) collective-permute-start(bf16[512,384]{1,0:T(8,128)(2,1)S(1)} %collective-permute-done.1.refs_4_), channel_id=1, source_target_pairs={{0,16},{16,0},{32,48},{48,32},{64,80},{80,64},{96,112},{112,96},{1... | collective-permute-start | bytes 1179656 | tf_op jit(solution)/shard_map/ppermute | solution.py:663
  60.5 3.8 %collective-permute-start.6 = (bf16[512,384]{1,0:T(8,128)(2,1)S(1)}, bf16[512,384]{1,0:T(8,128)(2,1)}, u32[]{:S(2)}, u32[]{:S(2)}) collective-permute-start(bf16[512,384]{1,0:T(8,128)(2,1)S(1)} %collective-permute-done.2.refs_6_), channel_id=1, source_target_pairs={{0,16},{16,0},{32,48},{48,32},{64,80},{80,64},{96,112},{112,96},{1... | collective-permute-start | bytes 1179656 | tf_op jit(solution)/shard_map/ppermute | solution.py:663
  60.5 3.8 %collective-permute-start.7 = (bf16[512,384]{1,0:T(8,128)(2,1)S(1)}, bf16[512,384]{1,0:T(8,128)(2,1)}, u32[]{:S(2)}, u32[]{:S(2)}) collective-permute-start(bf16[512,384]{1,0:T(8,128)(2,1)S(1)} %collective-permute-done.3.refs_8_), channel_id=1, source_target_pairs={{0,16},{16,0},{32,48},{48,32},{64,80},{80,64},{96,112},{112,96},{1... | collective-permute-start | bytes 1179656 | tf_op jit(solution)/shard_map/ppermute | solution.py:663
  63.8 11.9 %collective-permute-start.8 = (bf16[16,512]{1,0:T(8,128)(2,1)S(1)}, bf16[16,512]{1,0:T(8,128)(2,1)S(1)}, u32[]{:S(2)}, u32[]{:S(2)}) collective-permute-start(bf16[16,512]{1,0:T(8,128)(2,1)S(1)} %get-tuple-element.42), channel_id=1, source_target_pairs={{0,1},{1,2},{2,3},{3,4},{4,5},{5,6},{6,7},{7,8},{8,9},{9,10},{10,1... | collective-permute-start | bytes 49160 | tf_op jit(solution)/shard_map/ppermute | solution.py:676
  75.7 23.3 %all-to-all-start.3 = ((bf16[128,32,128]{2,1,0:T(8,128)(2,1)}), bf16[128,32,128]{2,1,0:T(8,128)(2,1)S(1)}, u32[]{:S(2)}, u32[]{:S(2)}) async-start(bf16[128,32,128]{2,1,0:T(8,128)(2,1)} %terms.1), calls=%async_computation.3 | async-start | bytes 2097152 | tf_op jit(solution)/shard_map/all_to_all | solution.py:680
